TPU v7x, 32 devices: a whole 2x2x4 slice. The times are simulated.
32 devices in a mesh: row: 4 (over y, core), col: 8 (over z, x).
Axes of the slice: x: 2, y: 2, z: 4, core: 2. Of those that a mesh axis runs over, the one named last changes fastest.
Arguments:
- act_sketch: bfloat16 [2, 2048, 256], P(None, 'row'), may hold values from -6 to 6
- grad_sketch: bfloat16 [2, 2048, 256], P(None, 'row'), may hold values from -6 to 6
- targets: float32 [2048, 256], P('row'), may hold values from -6 to 6
Outputs:
- residual: float32 [2048, 256], P(('row', 'col'))
All inputs are finite; a program needn't handle non-finite values.
Results may differ from a plain program's by a relative error of at most 0.014.
The roundings to bfloat16 on the way count: a program that leaves them out, or rounds other values in their place, can miss the bound.
Values may be sent and summed in bfloat16 or wider, within the bound.
No kernel may reach another device: no remote copies, remote signals or barrier semaphores. Data moves between devices by JAX's collectives and lax.ppermute only.
A program may use at most 64 MiB of HBM per device.

v0:
```python
import math

import jax
import jax.numpy as jnp
from jax import lax
from jax.sharding import PartitionSpec as P

ITERS = 8


def broadcast(value, axis, source):
    kept = jnp.where(lax.axis_index(axis) == source, value, 0).astype(value.dtype)
    return lax.psum(kept, axis)


def spread(panel, root):
    return broadcast(panel, "row", root)


def gram_pair(left, right):
    return lax.dot_general(
        left, right, (((1,), (1,)), ((), ())), preferred_element_type=jnp.float32
    )


def body(act_sketch, grad_sketch, targets):
    row_count = lax.axis_size("row")
    col_count = lax.axis_size("col")
    ratio = col_count // row_count
    examples = targets.shape[0]
    col_block = examples // ratio
    share_rows = examples // col_count
    col_place = lax.axis_index("col")
    root = col_place // ratio
    offset = col_place % ratio * col_block
    scale = act_sketch.shape[2] * math.sqrt(examples * row_count) / 4.0

    def pick(array, dim):
        return lax.dynamic_slice_in_dim(array, offset, col_block, dim)

    act_cols, grad_cols = (
        broadcast(pick(act_sketch, 1), "row", root),
        broadcast(pick(grad_sketch, 1), "row", root),
    )
    total = jnp.zeros((examples, col_block), jnp.float32)
    for layer in range(act_sketch.shape[0]):
        act_gram = gram_pair(act_sketch[layer], act_cols[layer])
        grad_gram = gram_pair(grad_sketch[layer], grad_cols[layer])
        total = total + act_gram * grad_gram
    kernel = (total / scale).astype(jnp.bfloat16)
    state = targets
    for step in range(ITERS):
        panel = spread(jnp.tanh(pick(state, 0)).astype(jnp.bfloat16), root)
        partial_value = jnp.dot(kernel, panel, preferred_element_type=jnp.float32)
        summed = lax.psum(partial_value, "col")
        state = state - 0.05 * summed
    return lax.dynamic_slice_in_dim(state, col_place * share_rows, share_rows, 0)


def solution(mesh):
    return jax.shard_map(
        body,
        mesh=mesh,
        in_specs=(P(None, "row", None), P(None, "row", None), P("row", None)),
        out_specs=P(("row", "col"), None),
        check_vma=False,
    )
```

profile of v0, /device:TPU:0, one launch (start us, length us, event | category | flops | bytes accessed | tf_op | source)
XLA Modules:
  0.0 893.2 jit_solution(1848905505805268601)
XLA Ops:
  6.5 1.6 fusion.13
  8.2 1.9 dynamic-slice_select_fusion
  10.2 36.9 %all-reduce.48.cloned.1.call-done = (bf16[2,256,256]{2,1,0:T(8,128)(2,1)}, bf16[2,256,256]{2,1,0:T(8,128)(2,1)}, bf16[256,256]{1,0:T(8,128)(2,1)}) async-done(((bf16[2,256,256]{2,1,0:T(8,128)(2,1)}, bf16[2,256,256]{2,1,0:T(8,128)(2,1)}, bf16[256,256]{1,0:T(8,128)(2,1)}), (bf16[2,256,256]{2,1,0:T(8,128)(2,1)}, bf16[2,256,256]{2,1,0:T(8,128)(2,1)}, bf16[256,256]{1,0:T(8,128)(2,1)})) %all-reduce.48.cloned.1.call-update) | async-done | bytes 655376 | tf_op jit(solution)/shard_map/psum | solution.py:13
  47.1 1.2 fusion.4
  51.7 72.5 %all-reduce.18.cloned.1.call-done = f32[512,256]{1,0:T(8,128)} async-done(((f32[512,256]{1,0:T(8,128)}), f32[512,256]{1,0:T(8,128)}) %all-reduce.18.cloned.1.call-update) | async-done | bytes 524304 | tf_op jit(solution)/shard_map/psum | solution.py:55
  124.2 1.1 multiply_subtract_fusion.6
  126.1 31.2 %all-reduce.20.cloned.1.call-done = bf16[256,256]{1,0:T(8,128)(2,1)} async-done(((bf16[256,256]{1,0:T(8,128)(2,1)}), bf16[256,256]{1,0:T(8,128)(2,1)}) %all-reduce.20.cloned.1.call-update) | async-done | bytes 131088 | tf_op jit(solution)/shard_map/psum | solution.py:13
  157.4 2.0 fusion.22
  159.4 73.6 %all-reduce.22.cloned.1.call-done = f32[512,256]{1,0:T(8,128)} async-done(((f32[512,256]{1,0:T(8,128)}), f32[512,256]{1,0:T(8,128)}) %all-reduce.22.cloned.1.call-update) | async-done | bytes 524304 | tf_op jit(solution)/shard_map/psum | solution.py:55
  233.0 1.1 multiply_subtract_fusion.5
  234.9 31.1 %all-reduce.24.cloned.1.call-done = bf16[256,256]{1,0:T(8,128)(2,1)} async-done(((bf16[256,256]{1,0:T(8,128)(2,1)}), bf16[256,256]{1,0:T(8,128)(2,1)}) %all-reduce.24.cloned.1.call-update) | async-done | bytes 131088 | tf_op jit(solution)/shard_map/psum | solution.py:13
  265.9 2.0 fusion.23
  268.0 73.6 %all-reduce.26.cloned.1.call-done = f32[512,256]{1,0:T(8,128)} async-done(((f32[512,256]{1,0:T(8,128)}), f32[512,256]{1,0:T(8,128)}) %all-reduce.26.cloned.1.call-update) | async-done | bytes 524304 | tf_op jit(solution)/shard_map/psum | solution.py:55
  341.6 1.1 multiply_subtract_fusion.4
  343.4 31.2 %all-reduce.28.cloned.1.call-done = bf16[256,256]{1,0:T(8,128)(2,1)} async-done(((bf16[256,256]{1,0:T(8,128)(2,1)}), bf16[256,256]{1,0:T(8,128)(2,1)}) %all-reduce.28.cloned.1.call-update) | async-done | bytes 131088 | tf_op jit(solution)/shard_map/psum | solution.py:13
  374.7 2.0 fusion.24
  376.7 73.7 %all-reduce.30.cloned.1.call-done = f32[512,256]{1,0:T(8,128)} async-done(((f32[512,256]{1,0:T(8,128)}), f32[512,256]{1,0:T(8,128)}) %all-reduce.30.cloned.1.call-update) | async-done | bytes 524304 | tf_op jit(solution)/shard_map/psum | solution.py:55
  450.4 1.1 multiply_subtract_fusion.3
  452.3 31.2 %all-reduce.32.cloned.1.call-done = bf16[256,256]{1,0:T(8,128)(2,1)} async-done(((bf16[256,256]{1,0:T(8,128)(2,1)}), bf16[256,256]{1,0:T(8,128)(2,1)}) %all-reduce.32.cloned.1.call-update) | async-done | bytes 131088 | tf_op jit(solution)/shard_map/psum | solution.py:13
  483.6 2.0 fusion.25
  485.6 73.6 %all-reduce.34.cloned.1.call-done = f32[512,256]{1,0:T(8,128)} async-done(((f32[512,256]{1,0:T(8,128)}), f32[512,256]{1,0:T(8,128)}) %all-reduce.34.cloned.1.call-update) | async-done | bytes 524304 | tf_op jit(solution)/shard_map/psum | solution.py:55
  561.1 31.2 %all-reduce.36.cloned.1.call-done = bf16[256,256]{1,0:T(8,128)(2,1)} async-done(((bf16[256,256]{1,0:T(8,128)(2,1)}), bf16[256,256]{1,0:T(8,128)(2,1)}) %all-reduce.36.cloned.1.call-update) | async-done | bytes 131088 | tf_op jit(solution)/shard_map/psum | solution.py:13
  592.3 2.0 fusion.26
  594.4 73.6 %all-reduce.38.cloned.1.call-done = f32[512,256]{1,0:T(8,128)} async-done(((f32[512,256]{1,0:T(8,128)}), f32[512,256]{1,0:T(8,128)}) %all-reduce.38.cloned.1.call-update) | async-done | bytes 524304 | tf_op jit(solution)/shard_map/psum | solution.py:55
  667.9 1.1 multiply_subtract_fusion.1
  669.8 31.2 %all-reduce.40.cloned.1.call-done = bf16[256,256]{1,0:T(8,128)(2,1)} async-done(((bf16[256,256]{1,0:T(8,128)(2,1)}), bf16[256,256]{1,0:T(8,128)(2,1)}) %all-reduce.40.cloned.1.call-update) | async-done | bytes 131088 | tf_op jit(solution)/shard_map/psum | solution.py:13
  701.0 2.0 fusion.27
  703.1 73.6 %all-reduce.42.cloned.1.call-done = f32[512,256]{1,0:T(8,128)} async-done(((f32[512,256]{1,0:T(8,128)}), f32[512,256]{1,0:T(8,128)}) %all-reduce.42.cloned.1.call-update) | async-done | bytes 524304 | tf_op jit(solution)/shard_map/psum | solution.py:55
  778.5 31.1 %all-reduce.44.cloned.1.call-done = bf16[256,256]{1,0:T(8,128)(2,1)} async-done(((bf16[256,256]{1,0:T(8,128)(2,1)}), bf16[256,256]{1,0:T(8,128)(2,1)}) %all-reduce.44.cloned.1.call-update) | async-done | bytes 131088 | tf_op jit(solution)/shard_map/psum | solution.py:13
  809.6 2.0 fusion.28
  811.6 73.6 %all-reduce.46.cloned.1.call-done = f32[512,256]{1,0:T(8,128)} async-done(((f32[512,256]{1,0:T(8,128)}), f32[512,256]{1,0:T(8,128)}) %all-reduce.46.cloned.1.call-update) | async-done | bytes 524304 | tf_op jit(solution)/shard_map/psum | solution.py:55
  885.2 1.5 dynamic-slice_subtract_fusion
  (57 shorter events, 11.3 us)
Async XLA Ops:
  6.5 40.5 %all-reduce.48.cloned.1.call-start = ((), (), s32[]{:S(2)}) async-start(), calls=%async_computation.15 | async-start | bytes 1310720 | tf_op jit(solution)/shard_map/psum | solution.py:13
  10.1 37.0 %copy-start = (bf16[2,512,256]{2,1,0:T(8,128)(2,1)S(1)}, bf16[2,512,256]{2,1,0:T(8,128)(2,1)}, u32[]{:S(2)}) copy-start(bf16[2,512,256]{2,1,0:T(8,128)(2,1)} %param.3) | copy-start | bytes 1572868
  10.1 114.1 %all-reduce.18.cloned.1.call-start = ((), (), s32[]{:S(2)}) async-start(), calls=%async_computation | async-start | bytes 1048576 | tf_op jit(solution)/shard_map/psum | solution.py:55
  47.1 1.2 copy-start.3
  48.3 1.0 copy-start.2
  48.3 1.1 copy-start.4
  49.7 0.9 copy-start.5
  50.6 73.6 %copy-start.1 = (f32[512,256]{1,0:T(8,128)S(1)}, f32[512,256]{1,0:T(8,128)}, u32[]{:S(2)}) copy-start(f32[512,256]{1,0:T(8,128)} %param.5) | copy-start | bytes 1572868
  51.7 105.7 %all-reduce.20.cloned.1.call-start = ((), (), s32[]{:S(2)}) async-start(), calls=%async_computation.1 | async-start | bytes 262144 | tf_op jit(solution)/shard_map/psum | solution.py:13
  126.1 106.9 %all-reduce.22.cloned.1.call-start = ((), (), s32[]{:S(2)}) async-start(), calls=%async_computation.2 | async-start | bytes 1048576 | tf_op jit(solution)/shard_map/psum | solution.py:55
  159.4 106.6 %all-reduce.24.cloned.1.call-start = ((), (), s32[]{:S(2)}) async-start(), calls=%async_computation.3 | async-start | bytes 262144 | tf_op jit(solution)/shard_map/psum | solution.py:13
  234.8 106.7 %all-reduce.26.cloned.1.call-start = ((), (), s32[]{:S(2)}) async-start(), calls=%async_computation.4 | async-start | bytes 1048576 | tf_op jit(solution)/shard_map/psum | solution.py:55
  267.9 106.7 %all-reduce.28.cloned.1.call-start = ((), (), s32[]{:S(2)}) async-start(), calls=%async_computation.5 | async-start | bytes 262144 | tf_op jit(solution)/shard_map/psum | solution.py:13
  343.4 107.1 %all-reduce.30.cloned.1.call-start = ((), (), s32[]{:S(2)}) async-start(), calls=%async_computation.6 | async-start | bytes 1048576 | tf_op jit(solution)/shard_map/psum | solution.py:55
  376.7 106.9 %all-reduce.32.cloned.1.call-start = ((), (), s32[]{:S(2)}) async-start(), calls=%async_computation.7 | async-start | bytes 262144 | tf_op jit(solution)/shard_map/psum | solution.py:13
  452.3 106.9 %all-reduce.34.cloned.1.call-start = ((), (), s32[]{:S(2)}) async-start(), calls=%async_computation.8 | async-start | bytes 1048576 | tf_op jit(solution)/shard_map/psum | solution.py:55
  485.6 106.8 %all-reduce.36.cloned.1.call-start = ((), (), s32[]{:S(2)}) async-start(), calls=%async_computation.9 | async-start | bytes 262144 | tf_op jit(solution)/shard_map/psum | solution.py:13
  561.0 106.9 %all-reduce.38.cloned.1.call-start = ((), (), s32[]{:S(2)}) async-start(), calls=%async_computation.10 | async-start | bytes 1048576 | tf_op jit(solution)/shard_map/psum | solution.py:55
  594.3 106.7 %all-reduce.40.cloned.1.call-start = ((), (), s32[]{:S(2)}) async-start(), calls=%async_computation.11 | async-start | bytes 262144 | tf_op jit(solution)/shard_map/psum | solution.py:13
  669.8 106.9 %all-reduce.42.cloned.1.call-start = ((), (), s32[]{:S(2)}) async-start(), calls=%async_computation.12 | async-start | bytes 1048576 | tf_op jit(solution)/shard_map/psum | solution.py:55
  703.0 106.6 %all-reduce.44.cloned.1.call-start = ((), (), s32[]{:S(2)}) async-start(), calls=%async_computation.13 | async-start | bytes 262144 | tf_op jit(solution)/shard_map/psum | solution.py:13
  778.5 106.7 %all-reduce.46.cloned.1.call-start = ((), (), s32[]{:S(2)}) async-start(), calls=%async_computation.14 | async-start | bytes 1048576 | tf_op jit(solution)/shard_map/psum | solution.py:55
Sparse Core Ops, SparseCore 0:
  10.2 36.7 all-reduce.47
  51.8 72.3 all-reduce.17
  126.7 30.6 all-reduce.19
  160.6 72.2 all-reduce.21
  235.2 30.6 all-reduce.23
  269.2 72.2 all-reduce.25
  344.0 30.6 all-reduce.27
  378.1 72.3 all-reduce.29
  452.9 30.6 all-reduce.31
  486.8 72.3 all-reduce.33
  561.6 30.6 all-reduce.35
  595.6 72.2 all-reduce.37
  670.4 30.6 all-reduce.39
  704.3 72.2 all-reduce.41
  778.9 30.6 all-reduce.43
  812.9 72.2 all-reduce.45
where the time goes:
time: 894 us; the launch traced here: 893 us
  waiting for transfers between devices  843 us (94%)
  other arithmetic  17.7 us (2%)
  matrix products  16.9 us (2%)
  between operations  13.4 us (1%)
    psum x8, waiting for transfers between devices, body(): summed = lax.psum(partial_value, 'col')  588 us
    psum x8, waiting for transfers between devices, broadcast(): return lax.psum(kept, axis)  255 us
  transfers between devices with their start and end apart: 16, of which 16 were waited for; matrix products, arithmetic and copies ran while one was open for 0% of the time, Pallas kernels for 0%

commit v1 on v0

--- a/solution.py
+++ b/solution.py
@@ -1,11 +1,18 @@
+import functools
 import math
 
 import jax
 import jax.numpy as jnp
 from jax import lax
+from jax.experimental import pallas as pl
+from jax.experimental.pallas import tpu as pltpu
 from jax.sharding import PartitionSpec as P
 
 ITERS = 8
+RATE = 0.05
+TILE = 256
+VMEM_LIMIT = 56 * 2**20
+NT = (((1,), (1,)), ((), ()))
 
 
 def broadcast(value, axis, source):
@@ -13,17 +20,11 @@
     return lax.psum(kept, axis)
 
 
-def spread(panel, root):
-    return broadcast(panel, "row", root)
-
-
 def gram_pair(left, right):
-    return lax.dot_general(
-        left, right, (((1,), (1,)), ((), ())), preferred_element_type=jnp.float32
-    )
-
-
-def body(act_sketch, grad_sketch, targets):
+    return lax.dot_general(left, right, NT, preferred_element_type=jnp.float32)
+
+
+def split_body(act_sketch, grad_sketch, targets):
     row_count = lax.axis_size("row")
     col_count = lax.axis_size("col")
     ratio = col_count // row_count
@@ -50,18 +51,171 @@
     kernel = (total / scale).astype(jnp.bfloat16)
     state = targets
     for step in range(ITERS):
-        panel = spread(jnp.tanh(pick(state, 0)).astype(jnp.bfloat16), root)
+        panel = broadcast(
+            jnp.tanh(pick(state, 0)).astype(jnp.bfloat16), "row", root
+        )
         partial_value = jnp.dot(kernel, panel, preferred_element_type=jnp.float32)
         summed = lax.psum(partial_value, "col")
-        state = state - 0.05 * summed
+        state = state - RATE * summed
     return lax.dynamic_slice_in_dim(state, col_place * share_rows, share_rows, 0)
 
 
+def pack_kernel(act, grad, targets, packed):
+    layers, _, width = act.shape
+    for layer in range(layers):
+        packed[:, layer * width : (layer + 1) * width] = act[layer]
+        packed[:, (layers + layer) * width : (layers + layer + 1) * width] = grad[layer]
+    value = targets[...]
+    high = value.astype(jnp.bfloat16)
+    out = value.shape[1]
+    at = 2 * layers * width
+    packed[:, at : at + out] = high
+    packed[:, at + out : at + 2 * out] = (value - high.astype(jnp.float32)).astype(
+        jnp.bfloat16
+    )
+
+
+def pack(act, grad, targets):
+    layers, rows, width = act.shape
+    out = targets.shape[1]
+    return pl.pallas_call(
+        pack_kernel,
+        out_shape=jax.ShapeDtypeStruct(
+            (rows, 2 * layers * width + 2 * out), jnp.bfloat16
+        ),
+        in_specs=[pl.BlockSpec(memory_space=pltpu.VMEM)] * 3,
+        out_specs=pl.BlockSpec(memory_space=pltpu.VMEM),
+        compiler_params=pltpu.CompilerParams(vmem_limit_bytes=VMEM_LIMIT),
+    )(act, grad, targets)
+
+
+def descent_kernel(layers, width, out, share, scale, pieces, *refs):
+    place = refs[0]
+    sources = refs[1 : 1 + pieces]
+    result = refs[1 + pieces]
+    data, kernel, residual, squashed, sems = refs[2 + pieces :]
+    examples = data.shape[0]
+    tiles = examples // TILE
+    copies, ends, at = [], [], 0
+    for index, source in enumerate(sources):
+        rows = source.shape[0]
+        copy = pltpu.make_async_copy(
+            source, data.at[pl.ds(at, rows), :], sems.at[index]
+        )
+        copy.start()
+        copies.append(copy)
+        at += rows
+        ends.append(at)
+
+    waited = 0
+    target_at = 2 * layers * width
+    for j in range(tiles):
+        cols = slice(j * TILE, (j + 1) * TILE)
+        while waited < pieces and (waited == 0 or ends[waited - 1] < (j + 1) * TILE):
+            copies[waited].wait()
+            waited += 1
+        value = data[cols, target_at : target_at + out].astype(jnp.float32) + data[
+            cols, target_at + out : target_at + 2 * out
+        ].astype(jnp.float32)
+        residual[cols, :] = value
+        squashed[0, cols, :] = jnp.tanh(value).astype(jnp.bfloat16)
+        for i in range(j + 1):
+            rows = slice(i * TILE, (i + 1) * TILE)
+            total = None
+            for layer in range(layers):
+                a = slice(layer * width, (layer + 1) * width)
+                g = slice((layers + layer) * width, (layers + layer + 1) * width)
+                term = gram_pair(data[rows, a], data[cols, a]) * gram_pair(
+                    data[rows, g], data[cols, g]
+                )
+                total = term if total is None else total + term
+            block = (total * (1.0 / scale)).astype(jnp.bfloat16)
+            kernel[rows, cols] = block
+            if i != j:
+                kernel[cols, rows] = block.T
+
+    for step in range(ITERS - 1):
+        now, later = step % 2, (step + 1) % 2
+        for i in range(tiles):
+            rows = slice(i * TILE, (i + 1) * TILE)
+            update = jnp.dot(
+                kernel[rows, :], squashed[now], preferred_element_type=jnp.float32
+            )
+            value = residual[rows, :] - RATE * update
+            residual[rows, :] = value
+            squashed[later, rows, :] = jnp.tanh(value).astype(jnp.bfloat16)
+    mine = pl.ds(pl.multiple_of(place[0] * share, share), share)
+    update = jnp.dot(
+        kernel[mine, :],
+        squashed[(ITERS - 1) % 2],
+        preferred_element_type=jnp.float32,
+    )
+    result[...] = residual[mine, :] - RATE * update
+
+
+def descend(place, sources, layers, width, out, share):
+    examples = sum(source.shape[0] for source in sources)
+    scale = width * math.sqrt(examples) / 4.0
+    pieces = len(sources)
+    return pl.pallas_call(
+        functools.partial(descent_kernel, layers, width, out, share, scale, pieces),
+        out_shape=jax.ShapeDtypeStruct((share, out), jnp.float32),
+        in_specs=[pl.BlockSpec(memory_space=pltpu.SMEM)]
+        + [pl.BlockSpec(memory_space=pl.ANY)] * pieces,
+        out_specs=pl.BlockSpec(memory_space=pltpu.VMEM),
+        scratch_shapes=[
+            pltpu.VMEM((examples, sources[0].shape[1]), jnp.bfloat16),
+            pltpu.VMEM((examples, examples), jnp.bfloat16),
+            pltpu.VMEM((examples, out), jnp.float32),
+            pltpu.VMEM((2, examples, out), jnp.bfloat16),
+            pltpu.SemaphoreType.DMA((pieces,)),
+        ],
+        compiler_params=pltpu.CompilerParams(vmem_limit_bytes=VMEM_LIMIT),
+    )(place, *sources)
+
+
+def whole_body(act_sketch, grad_sketch, targets):
+    row_count = lax.axis_size("row")
+    col_count = lax.axis_size("col")
+    layers, rows, width = act_sketch.shape
+    out = targets.shape[1]
+    packed = pack(act_sketch, grad_sketch, targets)
+
+    def twin(value):
+        return lax.ppermute(value, "row", [(i, i ^ 1) for i in range(row_count)])
+
+    pieces = [packed, twin(packed)]
+    for hop in range(2, row_count, 2):
+        other = lax.ppermute(
+            packed, "row", [(i, (i + hop) % row_count) for i in range(row_count)]
+        )
+        pieces += [other, twin(other)]
+    place = lax.axis_index("col").astype(jnp.int32).reshape(1)
+    return descend(place, pieces, layers, width, out, rows // col_count)
+
+
+def fits(mesh, act_sketch, targets):
+    layers, examples, width = act_sketch.shape
+    out = targets.shape[1]
+    share = examples // (mesh.shape["row"] * mesh.shape["col"])
+    held = examples * (2 * examples + 4 * layers * width + 12 * out)
+    return (
+        held <= VMEM_LIMIT * 3 // 4
+        and mesh.shape["row"] % 2 == 0
+        and examples // mesh.shape["row"] % TILE == 0
+        and share % 16 == 0
+    )
+
+
 def solution(mesh):
-    return jax.shard_map(
-        body,
-        mesh=mesh,
-        in_specs=(P(None, "row", None), P(None, "row", None), P("row", None)),
-        out_specs=P(("row", "col"), None),
-        check_vma=False,
-    )
+    def step(act_sketch, grad_sketch, targets):
+        body = whole_body if fits(mesh, act_sketch, targets) else split_body
+        return jax.shard_map(
+            body,
+            mesh=mesh,
+            in_specs=(P(None, "row", None), P(None, "row", None), P("row", None)),
+            out_specs=P(("row", "col"), None),
+            check_vma=False,
+        )(act_sketch, grad_sketch, targets)
+
+    return step

time: 894 us -> 67.9 us (0.08)
  waiting for transfers between devices: 843 us -> 38.1 us
  Pallas kernels: 0 us -> 26.5 us
  other arithmetic: 17.7 us -> 0 us
  matrix products: 16.9 us -> 0 us
  between operations: 13.4 us -> 0.18 us
    psum x16 -> x0, waiting for transfers between devices: 843 us -> none  [the longest x8 588 us: body(): summed = lax.psum(partial_value, 'col')]
    ppermute x0 -> x3, waiting for transfers between devices: none -> 38.1 us  [the longest x1 34.6 us: whole_body(): lax.ppermute(packed, 'row', [(i, (i + hop) % row_count) for i in range(ro...]
    pallas_call x0 -> x2, Pallas kernels: none -> 26.5 us  [the longest x1 23.8 us: descend(): pl.pallas_call(functools.partial(descent_kernel, layers, width, out, shar...]
    dot_general x12 -> x0, matrix products: 16.9 us -> none  [the longest x8 14.8 us: body(): partial_value = jnp.dot(kernel, panel, preferred_element_type=jnp.float32)]
    sub x8 -> x0, other arithmetic: 9.24 us -> none  [body(): state = state - 0.05 * summed]
  transfers between devices with their start and end apart: 16 -> 3, of which waited for: 16 -> 2; matrix products, arithmetic and copies ran while one was open for 0% -> 0% of each run, Pallas kernels for 0% -> 0%
where the time goes in v1:
time: 67.9 us; the launch traced here: 67.8 us
  waiting for transfers between devices  38.1 us (56%)
  Pallas kernels  26.5 us (39%)
  starting transfers between devices  2.97 us (4%)
    ppermute x1, waiting for transfers between devices, whole_body(): lax.ppermute(packed, 'row', [(i, (i + hop) % row_count) for i in range(ro...  34.6 us
    pallas_call x1, Pallas kernels, descend(): pl.pallas_call(functools.partial(descent_kernel, layers, width, out, shar...  23.8 us
    ppermute x2, waiting for transfers between devices, twin(): return lax.ppermute(value, 'row', [(i, i ^ 1) for i in range(row_count)])  3.53 us
    ppermute x1, starting transfers between devices, whole_body(): lax.ppermute(packed, 'row', [(i, (i + hop) % row_count) for i in range(ro...  2.97 us
    pallas_call x1, Pallas kernels, pack(): pl.pallas_call(pack_kernel, out_shape=jax.ShapeDtypeStruct((rows, 2 * lay...  2.69 us
  transfers between devices with their start and end apart: 3, of which 2 were waited for; matrix products, arithmetic and copies ran while one was open for 0% of the time, Pallas kernels for 0%

profile of v1, /device:TPU:0, one launch (start us, length us, event | category | flops | bytes accessed | tf_op | source)
XLA Modules:
  0.0 67.8 jit_solution(12886416954666548178)
XLA Ops:
  0.0 2.7 %shard_map.37.refs_1_ = bf16[512,1536]{1,0:T(8,128)(2,1)} custom-call(bf16[2,512,256]{2,1,0:T(8,128)(2,1)} %act.1, bf16[2,512,256]{2,1,0:T(8,128)(2,1)} %grad.1, f32[512,256]{1,0:T(8,128)} %targets.1), custom_call_target="tpu_custom_call" | custom-call | tf_op jit(solution)/shard_map/pallas_call | solution.py:81
  2.7 3.0 %collective-permute-start.1 = (bf16[512,1536]{1,0:T(8,128)(2,1)}, bf16[512,1536]{1,0:T(8,128)(2,1)S(1)}, u32[]{:S(2)}, u32[]{:S(2)}) collective-permute-start(bf16[512,1536]{1,0:T(8,128)(2,1)} %shard_map.37.refs_1_), channel_id=1, source_target_pairs={{0,16},{8,24},{16,0},{24,8},{1,17},{9,25},{17,1},{25,9},{2,18},{10... | collective-permute-start | bytes 4718600 | tf_op jit(solution)/shard_map/ppermute | solution.py:189
  5.7 0.0 collective-permute-start
  5.7 34.6 %collective-permute-done.1.refs_3_ = bf16[512,1536]{1,0:T(8,128)(2,1)S(1)} collective-permute-done((bf16[512,1536]{1,0:T(8,128)(2,1)}, bf16[512,1536]{1,0:T(8,128)(2,1)S(1)}, u32[]{:S(2)}, u32[]{:S(2)}) %collective-permute-start.1) | collective-permute-done | bytes 1572896 | tf_op jit(solution)/shard_map/ppermute | solution.py:189
  40.3 0.0 copy-start
  40.3 0.0 collective-permute-start.2
  40.3 0.0 collective-permute-done.refs_2_
  40.3 0.0 copy-start.1
  40.3 3.5 %collective-permute-done.2.refs_4_ = bf16[512,1536]{1,0:T(8,128)(2,1)} collective-permute-done((bf16[512,1536]{1,0:T(8,128)(2,1)S(1)}, bf16[512,1536]{1,0:T(8,128)(2,1)}, u32[]{:S(2)}, u32[]{:S(2)}) %collective-permute-start.2) | collective-permute-done | bytes 1572896 | tf_op jit(solution)/shard_map/ppermute | solution.py:185
  43.8 0.0 copy-done
  43.8 0.0 copy-done.1
  43.8 23.8 %shard_map.38 = f32[64,256]{1,0:T(8,128)} custom-call(s32[1]{0:T(128)} %bitcast.refs_0_, bf16[512,1536]{1,0:T(8,128)(2,1)} %shard_map.37.refs_1_, bf16[512,1536]{1,0:T(8,128)(2,1)} %copy-done.1, bf16[512,1536]{1,0:T(8,128)(2,1)} %copy-done, bf16[512,1536]{1,0:T(8,128)(2,1)} %collective-permute-done.2.refs_4_), custom_call_target="tpu_custom_call" | custom-call | tf_op jit(solution)/shard_map/pallas_call | solution.py:160
Async XLA Ops:
  2.7 37.6 %collective-permute-start.1 = (bf16[512,1536]{1,0:T(8,128)(2,1)}, bf16[512,1536]{1,0:T(8,128)(2,1)S(1)}, u32[]{:S(2)}, u32[]{:S(2)}) collective-permute-start(bf16[512,1536]{1,0:T(8,128)(2,1)} %shard_map.37.refs_1_), channel_id=1, source_target_pairs={{0,16},{8,24},{16,0},{24,8},{1,17},{9,25},{17,1},{25,9},{2,18},{10... | collective-permute-start | bytes 4718600 | tf_op jit(solution)/shard_map/ppermute | solution.py:189
  5.7 34.6 %collective-permute-start = (bf16[512,1536]{1,0:T(8,128)(2,1)}, bf16[512,1536]{1,0:T(8,128)(2,1)S(1)}, u32[]{:S(2)}, u32[]{:S(2)}) collective-permute-start(bf16[512,1536]{1,0:T(8,128)(2,1)} %shard_map.37.refs_1_), channel_id=1, source_target_pairs={{0,8},{8,0},{16,24},{24,16},{1,9},{9,1},{17,25},{25,17},{2,10},{10... | collective-permute-start | bytes 4718600 | tf_op jit(solution)/shard_map/ppermute | solution.py:185
  40.3 3.5 %copy-start = (bf16[512,1536]{1,0:T(8,128)(2,1)}, bf16[512,1536]{1,0:T(8,128)(2,1)S(1)}, u32[]{:S(2)}) copy-start(bf16[512,1536]{1,0:T(8,128)(2,1)S(1)} %collective-permute-done.1.refs_3_) | copy-start | bytes 4718596
  40.3 3.5 %collective-permute-start.2 = (bf16[512,1536]{1,0:T(8,128)(2,1)S(1)}, bf16[512,1536]{1,0:T(8,128)(2,1)}, u32[]{:S(2)}, u32[]{:S(2)}) collective-permute-start(bf16[512,1536]{1,0:T(8,128)(2,1)S(1)} %collective-permute-done.1.refs_3_), channel_id=1, source_target_pairs={{0,8},{8,0},{16,24},{24,16},{1,9},{9,1},{17,25},{25,17},{2,10},{10... | collective-permute-start | bytes 4718600 | tf_op jit(solution)/shard_map/ppermute | solution.py:185
  40.3 3.5 %copy-start.1 = (bf16[512,1536]{1,0:T(8,128)(2,1)}, bf16[512,1536]{1,0:T(8,128)(2,1)S(1)}, u32[]{:S(2)}) copy-start(bf16[512,1536]{1,0:T(8,128)(2,1)S(1)} %collective-permute-done.refs_2_) | copy-start | bytes 4718596

commit v2 on v0

v2 whole, which is shorter than its diff:
```python
import functools
import math

import jax
import jax.numpy as jnp
from jax import lax
from jax.experimental import pallas as pl
from jax.experimental.pallas import tpu as pltpu
from jax.sharding import PartitionSpec as P

ITERS = 8
RATE = 0.05
TILE = 256
STATE_LIMIT = 32 * 2**20
SCOPED_LIMIT = 16 * 2**20
NT = (((1,), (1,)), ((), ()))


def broadcast(value, axis, source):
    kept = jnp.where(lax.axis_index(axis) == source, value, 0).astype(value.dtype)
    return lax.psum(kept, axis)


def gram_pair(left, right):
    return lax.dot_general(left, right, NT, preferred_element_type=jnp.float32)


def split_body(act_sketch, grad_sketch, targets):
    row_count = lax.axis_size("row")
    col_count = lax.axis_size("col")
    ratio = col_count // row_count
    examples = targets.shape[0]
    col_block = examples // ratio
    share_rows = examples // col_count
    col_place = lax.axis_index("col")
    root = col_place // ratio
    offset = col_place % ratio * col_block
    scale = act_sketch.shape[2] * math.sqrt(examples * row_count) / 4.0

    def pick(array, dim):
        return lax.dynamic_slice_in_dim(array, offset, col_block, dim)

    act_cols, grad_cols = (
        broadcast(pick(act_sketch, 1), "row", root),
        broadcast(pick(grad_sketch, 1), "row", root),
    )
    total = jnp.zeros((examples, col_block), jnp.float32)
    for layer in range(act_sketch.shape[0]):
        act_gram = gram_pair(act_sketch[layer], act_cols[layer])
        grad_gram = gram_pair(grad_sketch[layer], grad_cols[layer])
        total = total + act_gram * grad_gram
    kernel = (total / scale).astype(jnp.bfloat16)
    state = targets
    for step in range(ITERS):
        panel = broadcast(
            jnp.tanh(pick(state, 0)).astype(jnp.bfloat16), "row", root
        )
        partial_value = jnp.dot(kernel, panel, preferred_element_type=jnp.float32)
        summed = lax.psum(partial_value, "col")
        state = state - RATE * summed
    return lax.dynamic_slice_in_dim(state, col_place * share_rows, share_rows, 0)


def kind_of(place):
    upper = (place // 2) % 2
    return (place % 2 + upper) % 2 * 2 + upper


def pack_kernel(takes, act, grad, targets, *refs):
    count = len(takes)
    packed, (token, wide, sem, wide_sem) = refs[:count], refs[count:]
    token[...] = jnp.zeros_like(token)
    layers, rows, width = act.shape
    out = targets.shape[1]
    quarter = rows // 4
    kind = kind_of(lax.axis_index("col"))
    copies, late, at = [], [], 0
    for ref, (flip, skip) in zip(packed, takes):
        size = ref.shape[0]
        quarter_at = (kind + flip - 2 * flip * (kind % 2)) * quarter + skip
        source = pl.ds(pl.multiple_of(quarter_at, 16), size)
        copy = pltpu.make_async_copy(
            targets.at[source, :], wide.at[pl.ds(at, size), :], wide_sem
        )
        copy.start()
        late.append(copy)
        at += size
        for layer in range(layers):
            for side, array in enumerate((act, grad)):
                lane = (side * layers + layer) * width
                copy = pltpu.make_async_copy(
                    array.at[layer, source, :], ref.at[:, pl.ds(lane, width)], sem
                )
                copy.start()
                copies.append(copy)
    for copy in late:
        copy.wait()
    at, lane = 0, 2 * layers * width
    for ref in packed:
        size = ref.shape[0]
        value = wide[at : at + size, :]
        high = value.astype(jnp.bfloat16)
        ref[:, lane : lane + out] = high
        ref[:, lane + out : lane + 2 * out] = (
            value - high.astype(jnp.float32)
        ).astype(jnp.bfloat16)
        at += size
    for copy in copies:
        copy.wait()


def pack(act, grad, targets, sizes, takes):
    layers, rows, width = act.shape
    out = targets.shape[1]
    lanes = 2 * layers * width + 2 * out
    return pl.pallas_call(
        functools.partial(pack_kernel, takes),
        out_shape=[jax.ShapeDtypeStruct((s, lanes), jnp.bfloat16) for s in sizes]
        + [TOKEN],
        in_specs=[pl.BlockSpec(memory_space=pltpu.HBM)] * 3,
        out_specs=[pl.BlockSpec(memory_space=pltpu.VMEM)] * (len(sizes) + 1),
        scratch_shapes=[
            pltpu.VMEM((sum(sizes), out), jnp.float32),
            pltpu.SemaphoreType.DMA(()),
            pltpu.SemaphoreType.DMA(()),
        ],
        compiler_params=pltpu.CompilerParams(vmem_limit_bytes=SCOPED_LIMIT),
    )(act, grad, targets)


def build(layers, scale, low, high, data, kernel):
    width = data.shape[1] // (2 * layers)
    for at in range(low, high, TILE):
        cols = slice(at, at + TILE)
        for row_at in range(0, at + TILE, TILE):
            rows = slice(row_at, row_at + TILE)
            total = None
            for layer in range(layers):
                a = slice(layer * width, (layer + 1) * width)
                g = slice((layers + layer) * width, (layers + layer + 1) * width)
                term = gram_pair(data[rows, a], data[cols, a]) * gram_pair(
                    data[rows, g], data[cols, g]
                )
                total = term if total is None else total + term
            block = (total * (1.0 / scale)).astype(jnp.bfloat16)
            kernel[rows, cols] = block
            if row_at != at:
                kernel[cols, rows] = block.T


def begin(low, high, kernel, residual, squashed):
    for at in range(low, high, TILE):
        cols = slice(at, at + TILE)
        squashed[cols, :] = jnp.tanh(residual[cols, :]).astype(jnp.bfloat16)
    for at in range(0, high, TILE):
        rows = slice(at, at + TILE)
        cols = slice(low if at < low else 0, high)
        residual[rows, :] -= RATE * jnp.dot(
            kernel[rows, cols], squashed[cols, :], preferred_element_type=jnp.float32
        )


def unpack_block(act, grad, low, data):
    layers, rows, width = act.shape
    for layer in range(layers):
        for side, array in enumerate((act, grad)):
            lane = (side * layers + layer) * width
            data[low : low + rows, lane : lane + width] = array[layer]


def unpack_pieces(pieces, low, data, residual):
    sketch, out = data.shape[1], residual.shape[1]
    for piece in pieces:
        high = low + piece.shape[0]
        data[low:high, :] = piece[:, :sketch]
        residual[low:high, :] = piece[:, sketch : sketch + out].astype(
            jnp.float32
        ) + piece[:, sketch + out :].astype(jnp.float32)
        low = high
    return low


def first_kernel(layers, scale, *refs):
    block, beside, state = refs[:3], refs[3:6], refs[7:11]
    token, sem = refs[11:]
    data, kernel, residual, squashed = state
    act, grad, targets = block
    rows, width = act.shape[1:]
    copies = [pltpu.make_async_copy(targets, residual.at[pl.ds(0, rows), :], sem)]
    for layer in range(layers):
        for side, array in enumerate((act, grad)):
            lane = (side * layers + layer) * width
            copies.append(
                pltpu.make_async_copy(
                    array.at[layer], data.at[pl.ds(0, rows), pl.ds(lane, width)], sem
                )
            )
    for copy in copies:
        copy.start()
    unpack_block(*beside[:2], rows, data)
    residual[rows : 2 * rows, :] = beside[2][...]
    for copy in copies:
        copy.wait()
    build(layers, scale, 0, 2 * rows, data, kernel)
    begin(0, 2 * rows, kernel, residual, squashed)
    token[...] = jnp.zeros_like(token)


def stage_kernel(layers, scale, low, count, *refs):
    pieces, state, token = refs[:count], refs[-5:-1], refs[-1]
    data, kernel, residual, squashed = state
    high = unpack_pieces(pieces, low, data, residual)
    build(layers, scale, low, high, data, kernel)
    begin(low, high, kernel, residual, squashed)
    token[...] = jnp.zeros_like(token)


def last_kernel(layers, scale, low, count, *refs):
    pieces, state = refs[:count], refs[count : count + 4]
    result, other = refs[count + 4 :]
    data, kernel, residual, squashed = state
    share = result.shape[0]
    high = unpack_pieces(pieces, low, data, residual)
    build(layers, scale, low, high, data, kernel)
    begin(low, high, kernel, residual, squashed)
    panels = (squashed, other)
    for at in range(0, high, TILE):
        rows = slice(at, at + TILE)
        other[rows, :] = jnp.tanh(residual[rows, :]).astype(jnp.bfloat16)
    for step in range(1, ITERS - 1):
        now, later = panels[step % 2], panels[(step + 1) % 2]
        for at in range(0, high, TILE):
            rows = slice(at, at + TILE)
            update = jnp.dot(
                kernel[rows, :], now[...], preferred_element_type=jnp.float32
            )
            value = residual[rows, :] - RATE * update
            residual[rows, :] = value
            later[rows, :] = jnp.tanh(value).astype(jnp.bfloat16)
    place = lax.axis_index("col")
    mine = pl.ds(pl.multiple_of(place * share, share), share)
    update = jnp.dot(
        kernel[mine, :],
        panels[(ITERS - 1) % 2][...],
        preferred_element_type=jnp.float32,
    )
    result[...] = residual[mine, :] - RATE * update


def hold_kernel(*refs):
    pass


IN_VMEM = pl.BlockSpec(memory_space=pltpu.VMEM)
IN_HBM = pl.BlockSpec(memory_space=pltpu.HBM)
PARAMS = pltpu.CompilerParams(vmem_limit_bytes=SCOPED_LIMIT)
SMALL = pltpu.CompilerParams(vmem_limit_bytes=SCOPED_LIMIT // 4)
TOKEN = jax.ShapeDtypeStruct((8, 128), jnp.float32)


def cost(layers, width, out, low, high):
    grown = high * high - low * low
    return pl.CostEstimate(
        flops=grown * (2 * layers * width + 2 * out),
        bytes_accessed=grown,
        transcendentals=(high - low) * out,
    )


def state_shapes(examples, sketch, out):
    return [
        pltpu.VMEM((examples, sketch), jnp.bfloat16),
        pltpu.VMEM((examples, examples), jnp.bfloat16),
        pltpu.VMEM((examples, out), jnp.float32),
        pltpu.VMEM((examples, out), jnp.bfloat16),
    ]


def after(value, *tokens):
    return pl.pallas_call(
        hold_kernel,
        out_shape=jax.ShapeDtypeStruct(value.shape, value.dtype),
        in_specs=[IN_HBM] * (1 + len(tokens)),
        out_specs=IN_HBM,
        input_output_aliases={0: 0},
        compiler_params=SMALL,
    )(value, *tokens)


def join_kernel(one, other, *refs):
    joined = refs[-1]
    rows = one.shape[0]
    joined[:rows, :] = one[...]
    joined[rows:, :] = other[...]


def join(one, other, *tokens):
    return pl.pallas_call(
        join_kernel,
        out_shape=jax.ShapeDtypeStruct((2 * one.shape[0], one.shape[1]), one.dtype),
        in_specs=[IN_VMEM] * 2 + [IN_HBM] * len(tokens),
        out_specs=IN_VMEM,
        compiler_params=SMALL,
    )(one, other, *tokens)


def whole_body(act_sketch, grad_sketch, targets):
    row_count = lax.axis_size("row")
    col_count = lax.axis_size("col")
    layers, rows, width = act_sketch.shape
    out = targets.shape[1]
    examples = rows * row_count
    share = rows // col_count
    scale = width * math.sqrt(examples) / 4.0
    quarter, eighth = rows // 4, rows // 8

    def twin(value):
        return lax.ppermute(value, "row", [(i, i ^ 1) for i in range(row_count)])

    def across(value):
        return lax.ppermute(value, "row", [(i, i ^ 2) for i in range(row_count)])

    def near(value):
        return lax.ppermute(value, "col", [(i, i ^ 1) for i in range(col_count)])

    def far(value):
        return lax.ppermute(value, "col", [(i, i ^ 2) for i in range(col_count)])

    shapes = state_shapes(examples, 2 * layers * width, out)

    def stage(state, low, pieces):
        count = len(pieces)
        *state, token = pl.pallas_call(
            functools.partial(stage_kernel, layers, scale, low, count),
            out_shape=[*shapes, TOKEN],
            in_specs=[IN_VMEM] * (count + 4),
            out_specs=[IN_VMEM] * 5,
            input_output_aliases={count + i: i for i in range(4)},
            compiler_params=PARAMS,
            cost_estimate=cost(layers, width, out, low, low + 2 * quarter),
        )(*pieces, *state)
        return state, token

    own = [
        pltpu.with_memory_space_constraint(array, pltpu.HBM)
        for array in (act_sketch, grad_sketch, targets)
    ]
    first, second, third, token = pack(
        *own,
        (eighth, eighth, quarter),
        ((0, 0), (0, eighth), (1, 0)),
    )
    first, second = across(first), across(second)
    beside = twin(act_sketch), twin(grad_sketch), twin(targets)
    third = across(after(third, *beside))
    *state, token = pl.pallas_call(
        functools.partial(first_kernel, layers, scale),
        out_shape=[*shapes, TOKEN],
        in_specs=[IN_HBM] * 3 + [IN_VMEM] * 3 + [IN_HBM],
        out_specs=[IN_VMEM] * 5,
        scratch_shapes=[pltpu.SemaphoreType.DMA(())],
        compiler_params=PARAMS,
        cost_estimate=cost(layers, width, out, 0, 2 * rows),
    )(*own, *beside, token)

    first, second = after(first, token), after(second, token)
    near_first, far_first = near(first), far(first)
    near_second, far_second = near(second), far(second)
    low = 2 * rows
    pieces = join(first, second, far_first)
    state, token = stage(state, low, [pieces, twin(pieces)])
    low += 2 * quarter
    pieces = join(near_first, far_first)
    state, token = stage(state, low, [pieces, twin(pieces)])
    low += 2 * quarter
    pieces = join(near_second, far_second, token)
    state, token = stage(state, low, [third, twin(third)])
    low += 2 * quarter
    pieces = [pieces, twin(pieces)]
    count = len(pieces)
    return pl.pallas_call(
        functools.partial(last_kernel, layers, scale, low, count),
        out_shape=jax.ShapeDtypeStruct((share, out), jnp.float32),
        in_specs=[IN_VMEM] * (count + 4),
        out_specs=IN_VMEM,
        scratch_shapes=[pltpu.VMEM((examples, out), jnp.bfloat16)],
        compiler_params=PARAMS,
    )(*pieces, *state)


def fits(mesh, act_sketch, targets):
    layers, examples, width = act_sketch.shape
    row_count, col_count = mesh.shape["row"], mesh.shape["col"]
    state = examples * (2 * examples + 4 * layers * width + 6 * targets.shape[1])
    return (
        state <= STATE_LIMIT
        and row_count == 4
        and col_count % 4 == 0
        and examples % (row_count * 2 * TILE) == 0
        and examples % (row_count * col_count * 16) == 0
    )


def solution(mesh):
    def step(act_sketch, grad_sketch, targets):
        body = whole_body if fits(mesh, act_sketch, targets) else split_body
        return jax.shard_map(
            body,
            mesh=mesh,
            in_specs=(P(None, "row", None), P(None, "row", None), P("row", None)),
            out_specs=P(("row", "col"), None),
            check_vma=False,
        )(act_sketch, grad_sketch, targets)

    return step
```

time: 894 us -> 47.7 us (0.05)
  waiting for transfers between devices: 843 us -> 7.87 us
  Pallas kernels: 0 us -> 27.8 us
  other arithmetic: 17.7 us -> 0 us
  matrix products: 16.9 us -> 0 us
  between operations: 13.4 us -> 0.09 us
  starting transfers between devices: 0.63 us -> 11.7 us
    psum x16 -> x0, waiting for transfers between devices: 843 us -> none  [the longest x8 588 us: body(): summed = lax.psum(partial_value, 'col')]
    pallas_call x0 -> x12, Pallas kernels: none -> 27.8 us  [the longest x1 17.4 us: whole_body(): pl.pallas_call(functools.partial(last_kernel, layers, scale, low, count),...]
    dot_general x12 -> x0, matrix products: 16.9 us -> none  [the longest x8 14.8 us: body(): partial_value = jnp.dot(kernel, panel, preferred_element_type=jnp.float32)]
    ppermute x0 -> x14, starting transfers between devices: none -> 11.7 us  [the longest x3 4.18 us: across(): return lax.ppermute(value, 'row', [(i, i ^ 2) for i in range(row_count)])]
    sub x8 -> x0, other arithmetic: 9.24 us -> none  [body(): state = state - 0.05 * summed]
  transfers between devices with their start and end apart: 16 -> 14, of which waited for: 16 -> 4; matrix products, arithmetic and copies ran while one was open for 0% -> 0% of each run, Pallas kernels for 0% -> 22%
where the time goes in v2:
time: 47.7 us; the launch traced here: 47.5 us
  Pallas kernels  27.8 us (58%)
  starting transfers between devices  11.7 us (25%)
  waiting for transfers between devices  7.87 us (16%)
    pallas_call x1, Pallas kernels, whole_body(): pl.pallas_call(functools.partial(last_kernel, layers, scale, low, count),...  17.4 us
    pallas_call x3, Pallas kernels, stage(): pl.pallas_call(functools.partial(stage_kernel, layers, scale, low, count)...  5.59 us
    ppermute x3, waiting for transfers between devices, across(): return lax.ppermute(value, 'row', [(i, i ^ 2) for i in range(row_count)])  5.1 us
    ppermute x3, starting transfers between devices, across(): return lax.ppermute(value, 'row', [(i, i ^ 2) for i in range(row_count)])  4.18 us
    pallas_call x1, Pallas kernels, whole_body(): pl.pallas_call(functools.partial(first_kernel, layers, scale), out_shape=...  3.5 us
    ppermute x2, starting transfers between devices, near(): return lax.ppermute(value, 'col', [(i, i ^ 1) for i in range(col_count)])  2.98 us
    ppermute x2, starting transfers between devices, far(): return lax.ppermute(value, 'col', [(i, i ^ 2) for i in range(col_count)])  2.88 us
    ppermute x7, starting transfers between devices, twin(): return lax.ppermute(value, 'row', [(i, i ^ 1) for i in range(row_count)])  1.69 us
  transfers between devices with their start and end apart: 14, of which 4 were waited for; matrix products, arithmetic and copies ran while one was open for 0% of the time, Pallas kernels for 22%

profile of v2, /device:TPU:0, one launch (start us, length us, event | category | flops | bytes accessed | tf_op | source)
XLA Modules:
  0.0 47.5 jit_solution(311303809609349207)
XLA Ops:
  0.0 0.5 collective-permute-start.1
  0.5 0.1 collective-permute-start.2
  0.5 0.5 collective-permute-start.3
  1.0 1.3 %shard_map.37 = (bf16[64,1536]{1,0:T(8,128)(2,1)S(1)}, bf16[64,1536]{1,0:T(8,128)(2,1)S(1)}, bf16[128,1536]{1,0:T(8,128)(2,1)S(1)}, f32[8,128]{1,0:T(8,128)S(1)}) custom-call(bf16[2,512,256]{2,1,0:T(8,128)(2,1)} %refs_0_.1, bf16[2,512,256]{2,1,0:T(8,128)(2,1)} %refs_1_.1, f32[512,256]{1,0:T(8,128)} %refs_2_.1), custom_call_target="tpu_custom_call" | custom-call | tf_op jit(solution)/shard_map/pallas_call | solution.py:116
  2.2 2.6 %collective-permute-start.6 = (bf16[64,1536]{1,0:T(8,128)(2,1)S(1)}, bf16[64,1536]{1,0:T(8,128)(2,1)S(1)}, u32[]{:S(2)}, u32[]{:S(2)}) collective-permute-start(bf16[64,1536]{1,0:T(8,128)(2,1)S(1)} %get-tuple-element.30), channel_id=1, source_target_pairs={{0,16},{8,24},{16,0},{24,8},{1,17},{9,25},{17,1},{25,9},{2,18},{10... | collective-permute-start | bytes 589832 | tf_op jit(solution)/shard_map/ppermute | solution.py:321
  4.8 0.1 collective-permute-start
  4.9 0.0 collective-permute-done.1.refs_3_.refs_1_
  4.9 0.0 collective-permute-done.2.refs_4_.refs_2_
  4.9 0.0 collective-permute-done.3.refs_5_.refs_3_
  4.9 3.5 %shard_map.38 = (bf16[2048,1024]{1,0:T(8,128)(2,1)S(1)}, bf16[2048,2048]{1,0:T(8,128)(2,1)S(1)}, f32[2048,256]{1,0:T(8,128)S(1)}, bf16[2048,256]{1,0:T(8,128)(2,1)S(1)}, f32[8,128]{1,0:T(8,128)S(1)}) custom-call(bf16[2,512,256]{2,1,0:T(8,128)(2,1)} %refs_0_.1, bf16[2,512,256]{2,1,0:T(8,128)(2,1)} %refs_1_.1, f32[512,256]{1,0:T(8,128)} %refs_2_.1, ...), custom_call_target="tpu_custom_call" | custom-call | flops 1610612736 | bytes 1048576 | tf_op jit(solution)/shard_map/pallas_call | solution.py:356
  8.4 2.2 %collective-permute-done.6.refs_0_ = bf16[64,1536]{1,0:T(8,128)(2,1)S(1)} collective-permute-done((bf16[64,1536]{1,0:T(8,128)(2,1)S(1)}, bf16[64,1536]{1,0:T(8,128)(2,1)S(1)}, u32[]{:S(2)}, u32[]{:S(2)}) %collective-permute-start.6) | collective-permute-done | bytes 196640 | tf_op jit(solution)/shard_map/ppermute | solution.py:321
  10.6 2.0 %collective-permute-start.8 = (bf16[64,1536]{1,0:T(8,128)(2,1)S(1)}, bf16[64,1536]{1,0:T(8,128)(2,1)S(1)}, u32[]{:S(2)}, u32[]{:S(2)}) collective-permute-start(bf16[64,1536]{1,0:T(8,128)(2,1)S(1)} %shard_map.40.one), channel_id=1, source_target_pairs={{0,2},{1,3},{2,0},{3,1},{4,6},{5,7},{6,4},{7,5},{8,10},{9,11},{10,... | collective-permute-start | bytes 589832 | tf_op jit(solution)/shard_map/ppermute | solution.py:327
  12.6 1.5 %collective-permute-start.7 = (bf16[64,1536]{1,0:T(8,128)(2,1)S(1)}, bf16[64,1536]{1,0:T(8,128)(2,1)S(1)}, u32[]{:S(2)}, u32[]{:S(2)}) collective-permute-start(bf16[64,1536]{1,0:T(8,128)(2,1)S(1)} %shard_map.40.one), channel_id=1, source_target_pairs={{0,1},{1,0},{2,3},{3,2},{4,5},{5,4},{6,7},{7,6},{8,9},{9,8},{10,11... | collective-permute-start | bytes 589832 | tf_op jit(solution)/shard_map/ppermute | solution.py:324
  14.1 1.5 %collective-permute-start.12 = (bf16[128,1536]{1,0:T(8,128)(2,1)S(1)}, bf16[128,1536]{1,0:T(8,128)(2,1)S(1)}, u32[]{:S(2)}, u32[]{:S(2)}) collective-permute-start(bf16[128,1536]{1,0:T(8,128)(2,1)S(1)} %shard_map.46), channel_id=1, source_target_pairs={{0,16},{8,24},{16,0},{24,8},{1,17},{9,25},{17,1},{25,9},{2,18},{10... | collective-permute-start | bytes 1179656 | tf_op jit(solution)/shard_map/ppermute | solution.py:321
  15.6 0.0 collective-permute-done.refs_0_
  15.6 1.5 %collective-permute-done.8.other.refs_0_ = bf16[64,1536]{1,0:T(8,128)(2,1)S(1)} collective-permute-done((bf16[64,1536]{1,0:T(8,128)(2,1)S(1)}, bf16[64,1536]{1,0:T(8,128)(2,1)S(1)}, u32[]{:S(2)}, u32[]{:S(2)}) %collective-permute-start.8) | collective-permute-done | bytes 196640 | tf_op jit(solution)/shard_map/ppermute | solution.py:327
  17.2 0.1 collective-permute-start.10
  17.2 1.2 %collective-permute-done.7.one = bf16[64,1536]{1,0:T(8,128)(2,1)S(1)} collective-permute-done((bf16[64,1536]{1,0:T(8,128)(2,1)S(1)}, bf16[64,1536]{1,0:T(8,128)(2,1)S(1)}, u32[]{:S(2)}, u32[]{:S(2)}) %collective-permute-start.7) | collective-permute-done | bytes 196640 | tf_op jit(solution)/shard_map/ppermute | solution.py:324
  18.5 0.1 collective-permute-start.9
  18.5 0.9 %collective-permute-start.5 = (bf16[64,1536]{1,0:T(8,128)(2,1)S(1)}, bf16[64,1536]{1,0:T(8,128)(2,1)S(1)}, u32[]{:S(2)}, u32[]{:S(2)}) collective-permute-start(bf16[64,1536]{1,0:T(8,128)(2,1)S(1)} %shard_map.39.other), channel_id=1, source_target_pairs={{0,2},{1,3},{2,0},{3,1},{4,6},{5,7},{6,4},{7,5},{8,10},{9,11},{10,... | collective-permute-start | bytes 589832 | tf_op jit(solution)/shard_map/ppermute | solution.py:327
  19.4 1.5 %collective-permute-start.4 = (bf16[64,1536]{1,0:T(8,128)(2,1)S(1)}, bf16[64,1536]{1,0:T(8,128)(2,1)S(1)}, u32[]{:S(2)}, u32[]{:S(2)}) collective-permute-start(bf16[64,1536]{1,0:T(8,128)(2,1)S(1)} %shard_map.39.other), channel_id=1, source_target_pairs={{0,1},{1,0},{2,3},{3,2},{4,5},{5,4},{6,7},{7,6},{8,9},{9,8},{10,11... | collective-permute-start | bytes 589832 | tf_op jit(solution)/shard_map/ppermute | solution.py:324
  20.9 2.9 %collective-permute-done.12.refs_0_ = bf16[128,1536]{1,0:T(8,128)(2,1)S(1)} collective-permute-done((bf16[128,1536]{1,0:T(8,128)(2,1)S(1)}, bf16[128,1536]{1,0:T(8,128)(2,1)S(1)}, u32[]{:S(2)}, u32[]{:S(2)}) %collective-permute-start.12) | collective-permute-done | bytes 393248 | tf_op jit(solution)/shard_map/ppermute | solution.py:321
  23.9 0.0 collective-permute-start.13
  23.9 0.0 collective-permute-done.10.refs_1_
  23.9 1.8 %shard_map.43 = (bf16[2048,1024]{1,0:T(8,128)(2,1)S(1)}, bf16[2048,2048]{1,0:T(8,128)(2,1)S(1)}, f32[2048,256]{1,0:T(8,128)S(1)}, bf16[2048,256]{1,0:T(8,128)(2,1)S(1)}, f32[8,128]{1,0:T(8,128)}) custom-call(bf16[128,1536]{1,0:T(8,128)(2,1)S(1)} %shard_map.42.refs_0_, ...), custom_call_target="tpu_custom_call", output_to_operand_aliasing={{0}: (2, {}), {1}: (3, {}), {2}: (4, {}), {3}: (5, {})} | custom-call | flops 905969664 | bytes 589824 | tf_op jit(solution)/shard_map/pallas_call | solution.py:333
  25.7 0.0 collective-permute-done.9.refs_1_
  25.7 1.5 %shard_map.44 = (bf16[2048,1024]{1,0:T(8,128)(2,1)S(1)}, bf16[2048,2048]{1,0:T(8,128)(2,1)S(1)}, f32[2048,256]{1,0:T(8,128)S(1)}, bf16[2048,256]{1,0:T(8,128)(2,1)S(1)}, f32[8,128]{1,0:T(8,128)S(1)}) custom-call(bf16[128,1536]{1,0:T(8,128)(2,1)S(1)} %shard_map.41.refs_0_, ...), custom_call_target="tpu_custom_call", output_to_operand_aliasing={{0}: (2, {}), {1}: (3, {}), {2}: (4, {}), {3}: (5, {})} | custom-call | flops 1107296256 | bytes 720896 | tf_op jit(solution)/shard_map/pallas_call | solution.py:333
  27.2 0.0 collective-permute-done.4.one
  27.2 0.6 %collective-permute-start.11 = (bf16[128,1536]{1,0:T(8,128)(2,1)S(1)}, bf16[128,1536]{1,0:T(8,128)(2,1)S(1)}, u32[]{:S(2)}, u32[]{:S(2)}) collective-permute-start(bf16[128,1536]{1,0:T(8,128)(2,1)S(1)} %shard_map.45.refs_0_), channel_id=1, source_target_pairs={{0,8},{8,0},{16,24},{24,16},{1,9},{9,1},{17,25},{25,17},{2,10},{10... | collective-permute-start | bytes 1179656 | tf_op jit(solution)/shard_map/ppermute | solution.py:318
  27.8 0.0 collective-permute-done.13.refs_1_
  27.8 2.3 %shard_map.47 = (bf16[2048,1024]{1,0:T(8,128)(2,1)S(1)}, bf16[2048,2048]{1,0:T(8,128)(2,1)S(1)}, f32[2048,256]{1,0:T(8,128)S(1)}, bf16[2048,256]{1,0:T(8,128)(2,1)S(1)}, f32[8,128]{1,0:T(8,128)}) custom-call(bf16[128,1536]{1,0:T(8,128)(2,1)S(1)} %collective-permute-done.12.refs_0_, ...), custom_call_target="tpu_custom_call", output_to_operand_aliasing={{0}: (2, {}), {1}: (3, {}), {2}: (4, {}), {3}: (5, {})} | custom-call | flops 1308622848 | bytes 851968 | tf_op jit(solution)/shard_map/pallas_call | solution.py:333
  30.1 17.4 %shard_map.48 = f32[64,256]{1,0:T(8,128)} custom-call(bf16[128,1536]{1,0:T(8,128)(2,1)S(1)} %shard_map.45.refs_0_, bf16[128,1536]{1,0:T(8,128)(2,1)S(1)} %collective-permute-done.11.refs_1_, bf16[2048,1024]{1,0:T(8,128)(2,1)S(1)} %get-tuple-element.45.refs_2_, bf16[2048,2048]{1,0:T(8,128)(2,1)S(1)} %get-tuple-element.46.refs_3_, ...), custom_call_target="tpu_custom_call" | custom-call | tf_op jit(solution)/shard_map/pallas_call | solution.py:381
  (8 shorter events, 0.1 us)
Async XLA Ops:
  0.0 4.9 %collective-permute-start.1 = (bf16[2,512,256]{2,1,0:T(8,128)(2,1)}, bf16[2,512,256]{2,1,0:T(8,128)(2,1)S(1)}, u32[]{:S(2)}, u32[]{:S(2)}) collective-permute-start(bf16[2,512,256]{2,1,0:T(8,128)(2,1)} %refs_0_.1), channel_id=1, source_target_pairs={{0,8},{8,0},{16,24},{24,16},{1,9},{9,1},{17,25},{25,17},{2,10},{10... | collective-permute-start | bytes 1572872 | tf_op jit(solution)/shard_map/ppermute | solution.py:318
  0.5 4.4 %collective-permute-start.2 = (bf16[2,512,256]{2,1,0:T(8,128)(2,1)}, bf16[2,512,256]{2,1,0:T(8,128)(2,1)S(1)}, u32[]{:S(2)}, u32[]{:S(2)}) collective-permute-start(bf16[2,512,256]{2,1,0:T(8,128)(2,1)} %refs_1_.1), channel_id=1, source_target_pairs={{0,8},{8,0},{16,24},{24,16},{1,9},{9,1},{17,25},{25,17},{2,10},{10... | collective-permute-start | bytes 1572872 | tf_op jit(solution)/shard_map/ppermute | solution.py:318
  0.5 4.4 %collective-permute-start.3 = (f32[512,256]{1,0:T(8,128)}, f32[512,256]{1,0:T(8,128)S(1)}, u32[]{:S(2)}, u32[]{:S(2)}) collective-permute-start(f32[512,256]{1,0:T(8,128)} %refs_2_.1), channel_id=1, source_target_pairs={{0,8},{8,0},{16,24},{24,16},{1,9},{9,1},{17,25},{25,17},{2,10},{10... | collective-permute-start | bytes 1572872 | tf_op jit(solution)/shard_map/ppermute | solution.py:318
  2.2 8.3 %collective-permute-start.6 = (bf16[64,1536]{1,0:T(8,128)(2,1)S(1)}, bf16[64,1536]{1,0:T(8,128)(2,1)S(1)}, u32[]{:S(2)}, u32[]{:S(2)}) collective-permute-start(bf16[64,1536]{1,0:T(8,128)(2,1)S(1)} %get-tuple-element.30), channel_id=1, source_target_pairs={{0,16},{8,24},{16,0},{24,8},{1,17},{9,25},{17,1},{25,9},{2,18},{10... | collective-permute-start | bytes 589832 | tf_op jit(solution)/shard_map/ppermute | solution.py:321
  4.8 10.8 %collective-permute-start = (bf16[64,1536]{1,0:T(8,128)(2,1)S(1)}, bf16[64,1536]{1,0:T(8,128)(2,1)S(1)}, u32[]{:S(2)}, u32[]{:S(2)}) collective-permute-start(bf16[64,1536]{1,0:T(8,128)(2,1)S(1)} %get-tuple-element.27), channel_id=1, source_target_pairs={{0,16},{8,24},{16,0},{24,8},{1,17},{9,25},{17,1},{25,9},{2,18},{10... | collective-permute-start | bytes 589832 | tf_op jit(solution)/shard_map/ppermute | solution.py:321
  10.6 6.6 %collective-permute-start.8 = (bf16[64,1536]{1,0:T(8,128)(2,1)S(1)}, bf16[64,1536]{1,0:T(8,128)(2,1)S(1)}, u32[]{:S(2)}, u32[]{:S(2)}) collective-permute-start(bf16[64,1536]{1,0:T(8,128)(2,1)S(1)} %shard_map.40.one), channel_id=1, source_target_pairs={{0,2},{1,3},{2,0},{3,1},{4,6},{5,7},{6,4},{7,5},{8,10},{9,11},{10,... | collective-permute-start | bytes 589832 | tf_op jit(solution)/shard_map/ppermute | solution.py:327
  12.6 5.9 %collective-permute-start.7 = (bf16[64,1536]{1,0:T(8,128)(2,1)S(1)}, bf16[64,1536]{1,0:T(8,128)(2,1)S(1)}, u32[]{:S(2)}, u32[]{:S(2)}) collective-permute-start(bf16[64,1536]{1,0:T(8,128)(2,1)S(1)} %shard_map.40.one), channel_id=1, source_target_pairs={{0,1},{1,0},{2,3},{3,2},{4,5},{5,4},{6,7},{7,6},{8,9},{9,8},{10,11... | collective-permute-start | bytes 589832 | tf_op jit(solution)/shard_map/ppermute | solution.py:324
  14.1 9.8 %collective-permute-start.12 = (bf16[128,1536]{1,0:T(8,128)(2,1)S(1)}, bf16[128,1536]{1,0:T(8,128)(2,1)S(1)}, u32[]{:S(2)}, u32[]{:S(2)}) collective-permute-start(bf16[128,1536]{1,0:T(8,128)(2,1)S(1)} %shard_map.46), channel_id=1, source_target_pairs={{0,16},{8,24},{16,0},{24,8},{1,17},{9,25},{17,1},{25,9},{2,18},{10... | collective-permute-start | bytes 1179656 | tf_op jit(solution)/shard_map/ppermute | solution.py:321
  17.2 6.7 %collective-permute-start.10 = (bf16[128,1536]{1,0:T(8,128)(2,1)S(1)}, bf16[128,1536]{1,0:T(8,128)(2,1)S(1)}, u32[]{:S(2)}, u32[]{:S(2)}) collective-permute-start(bf16[128,1536]{1,0:T(8,128)(2,1)S(1)} %shard_map.42.refs_0_), channel_id=1, source_target_pairs={{0,8},{8,0},{16,24},{24,16},{1,9},{9,1},{17,25},{25,17},{2,10},{10... | collective-permute-start | bytes 1179656 | tf_op jit(solution)/shard_map/ppermute | solution.py:318
  18.5 7.2 %collective-permute-start.9 = (bf16[128,1536]{1,0:T(8,128)(2,1)S(1)}, bf16[128,1536]{1,0:T(8,128)(2,1)S(1)}, u32[]{:S(2)}, u32[]{:S(2)}) collective-permute-start(bf16[128,1536]{1,0:T(8,128)(2,1)S(1)} %shard_map.41.refs_0_), channel_id=1, source_target_pairs={{0,8},{8,0},{16,24},{24,16},{1,9},{9,1},{17,25},{25,17},{2,10},{10... | collective-permute-start | bytes 1179656 | tf_op jit(solution)/shard_map/ppermute | solution.py:318
  18.5 8.6 %collective-permute-start.5 = (bf16[64,1536]{1,0:T(8,128)(2,1)S(1)}, bf16[64,1536]{1,0:T(8,128)(2,1)S(1)}, u32[]{:S(2)}, u32[]{:S(2)}) collective-permute-start(bf16[64,1536]{1,0:T(8,128)(2,1)S(1)} %shard_map.39.other), channel_id=1, source_target_pairs={{0,2},{1,3},{2,0},{3,1},{4,6},{5,7},{6,4},{7,5},{8,10},{9,11},{10,... | collective-permute-start | bytes 589832 | tf_op jit(solution)/shard_map/ppermute | solution.py:327
  19.4 7.8 %collective-permute-start.4 = (bf16[64,1536]{1,0:T(8,128)(2,1)S(1)}, bf16[64,1536]{1,0:T(8,128)(2,1)S(1)}, u32[]{:S(2)}, u32[]{:S(2)}) collective-permute-start(bf16[64,1536]{1,0:T(8,128)(2,1)S(1)} %shard_map.39.other), channel_id=1, source_target_pairs={{0,1},{1,0},{2,3},{3,2},{4,5},{5,4},{6,7},{7,6},{8,9},{9,8},{10,11... | collective-permute-start | bytes 589832 | tf_op jit(solution)/shard_map/ppermute | solution.py:324
  23.9 4.0 %collective-permute-start.13 = (bf16[128,1536]{1,0:T(8,128)(2,1)S(1)}, bf16[128,1536]{1,0:T(8,128)(2,1)S(1)}, u32[]{:S(2)}, u32[]{:S(2)}) collective-permute-start(bf16[128,1536]{1,0:T(8,128)(2,1)S(1)} %collective-permute-done.12.refs_0_), channel_id=1, source_target_pairs={{0,8},{8,0},{16,24},{24,16},{1,9},{9,1},{17,25},{25,17},{2,10},{10... | collective-permute-start | bytes 1179656 | tf_op jit(solution)/shard_map/ppermute | solution.py:318
  27.2 2.9 %collective-permute-start.11 = (bf16[128,1536]{1,0:T(8,128)(2,1)S(1)}, bf16[128,1536]{1,0:T(8,128)(2,1)S(1)}, u32[]{:S(2)}, u32[]{:S(2)}) collective-permute-start(bf16[128,1536]{1,0:T(8,128)(2,1)S(1)} %shard_map.45.refs_0_), channel_id=1, source_target_pairs={{0,8},{8,0},{16,24},{24,16},{1,9},{9,1},{17,25},{25,17},{2,10},{10... | collective-permute-start | bytes 1179656 | tf_op jit(solution)/shard_map/ppermute | solution.py:318

commit v3 on v2

--- a/solution.py
+++ b/solution.py
@@ -222,11 +222,17 @@
     share = result.shape[0]
     high = unpack_pieces(pieces, low, data, residual)
     build(layers, scale, low, high, data, kernel)
-    begin(low, high, kernel, residual, squashed)
+    for at in range(low, high, TILE):
+        cols = slice(at, at + TILE)
+        squashed[cols, :] = jnp.tanh(residual[cols, :]).astype(jnp.bfloat16)
+    for at in range(0, high, TILE):
+        rows, cols = slice(at, at + TILE), slice(low if at < low else 0, high)
+        value = residual[rows, :] - RATE * jnp.dot(
+            kernel[rows, cols], squashed[cols, :], preferred_element_type=jnp.float32
+        )
+        residual[rows, :] = value
+        other[rows, :] = jnp.tanh(value).astype(jnp.bfloat16)
     panels = (squashed, other)
-    for at in range(0, high, TILE):
-        rows = slice(at, at + TILE)
-        other[rows, :] = jnp.tanh(residual[rows, :]).astype(jnp.bfloat16)
     for step in range(1, ITERS - 1):
         now, later = panels[step % 2], panels[(step + 1) % 2]
         for at in range(0, high, TILE):
@@ -287,21 +293,22 @@
     )(value, *tokens)
 
 
-def join_kernel(one, other, *refs):
-    joined = refs[-1]
-    rows = one.shape[0]
-    joined[:rows, :] = one[...]
-    joined[rows:, :] = other[...]
-
-
-def join(one, other, *tokens):
+def join_kernel(count, *refs):
+    joined, at = refs[-1], 0
+    for piece in refs[:count]:
+        joined[at : at + piece.shape[0], :] = piece[...]
+        at += piece.shape[0]
+
+
+def join(pieces, *tokens):
+    shape = sum(piece.shape[0] for piece in pieces), pieces[0].shape[1]
     return pl.pallas_call(
-        join_kernel,
-        out_shape=jax.ShapeDtypeStruct((2 * one.shape[0], one.shape[1]), one.dtype),
-        in_specs=[IN_VMEM] * 2 + [IN_HBM] * len(tokens),
+        functools.partial(join_kernel, len(pieces)),
+        out_shape=jax.ShapeDtypeStruct(shape, pieces[0].dtype),
+        in_specs=[IN_VMEM] * len(pieces) + [IN_HBM] * len(tokens),
         out_specs=IN_VMEM,
         compiler_params=SMALL,
-    )(one, other, *tokens)
+    )(*pieces, *tokens)
 
 
 def whole_body(act_sketch, grad_sketch, targets):
@@ -328,17 +335,16 @@
 
     shapes = state_shapes(examples, 2 * layers * width, out)
 
-    def stage(state, low, pieces):
+    def stage(state, low, pieces, *tokens):
         count = len(pieces)
         *state, token = pl.pallas_call(
             functools.partial(stage_kernel, layers, scale, low, count),
             out_shape=[*shapes, TOKEN],
-            in_specs=[IN_VMEM] * (count + 4),
+            in_specs=[IN_VMEM] * (count + 4) + [IN_HBM] * len(tokens),
             out_specs=[IN_VMEM] * 5,
             input_output_aliases={count + i: i for i in range(4)},
             compiler_params=PARAMS,
-            cost_estimate=cost(layers, width, out, low, low + 2 * quarter),
-        )(*pieces, *state)
+        )(*pieces, *state, *tokens)
         return state, token
 
     own = [
@@ -352,7 +358,7 @@
     )
     first, second = across(first), across(second)
     beside = twin(act_sketch), twin(grad_sketch), twin(targets)
-    third = across(after(third, *beside))
+    third = across(third)
     *state, token = pl.pallas_call(
         functools.partial(first_kernel, layers, scale),
         out_shape=[*shapes, TOKEN],
@@ -367,15 +373,14 @@
     near_first, far_first = near(first), far(first)
     near_second, far_second = near(second), far(second)
     low = 2 * rows
-    pieces = join(first, second, far_first)
-    state, token = stage(state, low, [pieces, twin(pieces)])
-    low += 2 * quarter
-    pieces = join(near_first, far_first)
-    state, token = stage(state, low, [pieces, twin(pieces)])
-    low += 2 * quarter
-    pieces = join(near_second, far_second, token)
+    four = [first, second, near_first, far_first]
+    state, token = stage(state, low, four + [twin(piece) for piece in four])
+    low += 4 * quarter
+    last = join([near_second, far_second], token)
+    third = after(third, token)
     state, token = stage(state, low, [third, twin(third)])
     low += 2 * quarter
+    pieces = last
     pieces = [pieces, twin(pieces)]
     count = len(pieces)
     return pl.pallas_call(

time: 47.7 us -> 45.8 us (0.960)
  Pallas kernels: 27.8 us -> 26.8 us
  waiting for transfers between devices: 7.87 us -> 7.15 us
    ppermute x3, waiting for transfers between devices: 5.1 us -> 2.83 us  [across(): return lax.ppermute(value, 'row', [(i, i ^ 2) for i in range(row_count)])]
    ppermute x2, waiting for transfers between devices: 1.21 us -> 2.83 us  [near(): return lax.ppermute(value, 'col', [(i, i ^ 1) for i in range(col_count)])]
    pallas_call x3 -> x2, Pallas kernels: 5.59 us -> 4.74 us  [stage(): pl.pallas_call(functools.partial(stage_kernel, layers, scale, low, count)...]
    ppermute x7 -> x9, starting transfers between devices: 1.69 us -> 1.55 us  [twin(): return lax.ppermute(value, 'row', [(i, i ^ 1) for i in range(row_count)])]
  transfers between devices with their start and end apart: 14 -> 16, of which waited for: 4 -> 6; matrix products, arithmetic and copies ran while one was open for 0% -> 0% of each run, Pallas kernels for 22% -> 21%
where the time goes in v3:
time: 45.8 us; the launch traced here: 45.6 us
  Pallas kernels  26.8 us (59%)
  starting transfers between devices  11.6 us (25%)
  waiting for transfers between devices  7.15 us (16%)
    pallas_call x1, Pallas kernels, whole_body(): pl.pallas_call(functools.partial(last_kernel, layers, scale, low, count),...  17.3 us
    pallas_call x2, Pallas kernels, stage(): pl.pallas_call(functools.partial(stage_kernel, layers, scale, low, count)...  4.74 us
    ppermute x3, starting transfers between devices, across(): return lax.ppermute(value, 'row', [(i, i ^ 2) for i in range(row_count)])  4.18 us
    pallas_call x1, Pallas kernels, whole_body(): pl.pallas_call(functools.partial(first_kernel, layers, scale), out_shape=...  3.5 us
    ppermute x2, starting transfers between devices, far(): return lax.ppermute(value, 'col', [(i, i ^ 2) for i in range(col_count)])  3.15 us
    ppermute x2, waiting for transfers between devices, near(): return lax.ppermute(value, 'col', [(i, i ^ 1) for i in range(col_count)])  2.83 us
    ppermute x3, waiting for transfers between devices, across(): return lax.ppermute(value, 'row', [(i, i ^ 2) for i in range(row_count)])  2.83 us
    ppermute x2, starting transfers between devices, near(): return lax.ppermute(value, 'col', [(i, i ^ 1) for i in range(col_count)])  2.71 us
  transfers between devices with their start and end apart: 16, of which 6 were waited for; matrix products, arithmetic and copies ran while one was open for 0% of the time, Pallas kernels for 21%

profile of v3, /device:TPU:0, one launch (start us, length us, event | category | flops | bytes accessed | tf_op | source)
XLA Modules:
  0.0 45.6 jit_solution(4708048253244657730)
XLA Ops:
  0.0 0.5 collective-permute-start.1
  0.5 0.1 collective-permute-start.2
  0.5 0.5 collective-permute-start.3
  1.0 1.3 %shard_map.37 = (bf16[64,1536]{1,0:T(8,128)(2,1)S(1)}, bf16[64,1536]{1,0:T(8,128)(2,1)S(1)}, bf16[128,1536]{1,0:T(8,128)(2,1)S(1)}, f32[8,128]{1,0:T(8,128)S(1)}) custom-call(bf16[2,512,256]{2,1,0:T(8,128)(2,1)} %refs_0_.1, bf16[2,512,256]{2,1,0:T(8,128)(2,1)} %refs_1_.1, f32[512,256]{1,0:T(8,128)} %refs_2_.1), custom_call_target="tpu_custom_call" | custom-call | tf_op jit(solution)/shard_map/pallas_call | solution.py:116
  2.2 2.6 %collective-permute-start.6 = (bf16[64,1536]{1,0:T(8,128)(2,1)S(1)}, bf16[64,1536]{1,0:T(8,128)(2,1)S(1)}, u32[]{:S(2)}, u32[]{:S(2)}) collective-permute-start(bf16[64,1536]{1,0:T(8,128)(2,1)S(1)} %get-tuple-element.26), channel_id=1, source_target_pairs={{0,16},{8,24},{16,0},{24,8},{1,17},{9,25},{17,1},{25,9},{2,18},{10... | collective-permute-start | bytes 589832 | tf_op jit(solution)/shard_map/ppermute | solution.py:328
  4.8 0.1 collective-permute-start
  4.9 0.0 collective-permute-done.1.refs_3_
  4.9 0.0 collective-permute-done.2.refs_4_
  4.9 0.0 collective-permute-done.3.refs_5_
  4.9 3.5 %shard_map.38 = (bf16[2048,1024]{1,0:T(8,128)(2,1)S(1)}, bf16[2048,2048]{1,0:T(8,128)(2,1)S(1)}, f32[2048,256]{1,0:T(8,128)S(1)}, bf16[2048,256]{1,0:T(8,128)(2,1)S(1)}, f32[8,128]{1,0:T(8,128)S(1)}) custom-call(bf16[2,512,256]{2,1,0:T(8,128)(2,1)} %refs_0_.1, bf16[2,512,256]{2,1,0:T(8,128)(2,1)} %refs_1_.1, f32[512,256]{1,0:T(8,128)} %refs_2_.1, ...), custom_call_target="tpu_custom_call" | custom-call | flops 1610612736 | bytes 1048576 | tf_op jit(solution)/shard_map/pallas_call | solution.py:362
  8.4 2.2 %collective-permute-done.6.refs_0_ = bf16[64,1536]{1,0:T(8,128)(2,1)S(1)} collective-permute-done((bf16[64,1536]{1,0:T(8,128)(2,1)S(1)}, bf16[64,1536]{1,0:T(8,128)(2,1)S(1)}, u32[]{:S(2)}, u32[]{:S(2)}) %collective-permute-start.6) | collective-permute-done | bytes 196640 | tf_op jit(solution)/shard_map/ppermute | solution.py:328
  10.6 1.9 %collective-permute-start.7 = (bf16[64,1536]{1,0:T(8,128)(2,1)S(1)}, bf16[64,1536]{1,0:T(8,128)(2,1)S(1)}, u32[]{:S(2)}, u32[]{:S(2)}) collective-permute-start(bf16[64,1536]{1,0:T(8,128)(2,1)S(1)} %shard_map.40.refs_0_), channel_id=1, source_target_pairs={{0,1},{1,0},{2,3},{3,2},{4,5},{5,4},{6,7},{7,6},{8,9},{9,8},{10,11... | collective-permute-start | bytes 589832 | tf_op jit(solution)/shard_map/ppermute | solution.py:331
  12.5 1.6 %collective-permute-start.8 = (bf16[64,1536]{1,0:T(8,128)(2,1)S(1)}, bf16[64,1536]{1,0:T(8,128)(2,1)S(1)}, u32[]{:S(2)}, u32[]{:S(2)}) collective-permute-start(bf16[64,1536]{1,0:T(8,128)(2,1)S(1)} %shard_map.40.refs_0_), channel_id=1, source_target_pairs={{0,2},{1,3},{2,0},{3,1},{4,6},{5,7},{6,4},{7,5},{8,10},{9,11},{10,... | collective-permute-start | bytes 589832 | tf_op jit(solution)/shard_map/ppermute | solution.py:334
  14.1 1.5 %collective-permute-start.14 = (bf16[128,1536]{1,0:T(8,128)(2,1)S(1)}, bf16[128,1536]{1,0:T(8,128)(2,1)S(1)}, u32[]{:S(2)}, u32[]{:S(2)}) collective-permute-start(bf16[128,1536]{1,0:T(8,128)(2,1)S(1)} %get-tuple-element.32), channel_id=1, source_target_pairs={{0,16},{8,24},{16,0},{24,8},{1,17},{9,25},{17,1},{25,9},{2,18},{10... | collective-permute-start | bytes 1179656 | tf_op jit(solution)/shard_map/ppermute | solution.py:328
  15.6 0.0 collective-permute-start.9
  15.6 0.5 %collective-permute-start.10 = (bf16[64,1536]{1,0:T(8,128)(2,1)S(1)}, bf16[64,1536]{1,0:T(8,128)(2,1)S(1)}, u32[]{:S(2)}, u32[]{:S(2)}) collective-permute-start(bf16[64,1536]{1,0:T(8,128)(2,1)S(1)} %shard_map.39.refs_1_), channel_id=1, source_target_pairs={{0,8},{8,0},{16,24},{24,16},{1,9},{9,1},{17,25},{25,17},{2,10},{10... | collective-permute-start | bytes 589832 | tf_op jit(solution)/shard_map/ppermute | solution.py:325
  16.1 1.0 %collective-permute-done.7.refs_2_ = bf16[64,1536]{1,0:T(8,128)(2,1)S(1)} collective-permute-done((bf16[64,1536]{1,0:T(8,128)(2,1)S(1)}, bf16[64,1536]{1,0:T(8,128)(2,1)S(1)}, u32[]{:S(2)}, u32[]{:S(2)}) %collective-permute-start.7) | collective-permute-done | bytes 196640 | tf_op jit(solution)/shard_map/ppermute | solution.py:331
  17.1 1.2 %collective-permute-done.8.refs_3_ = bf16[64,1536]{1,0:T(8,128)(2,1)S(1)} collective-permute-done((bf16[64,1536]{1,0:T(8,128)(2,1)S(1)}, bf16[64,1536]{1,0:T(8,128)(2,1)S(1)}, u32[]{:S(2)}, u32[]{:S(2)}) %collective-permute-start.8) | collective-permute-done | bytes 196640 | tf_op jit(solution)/shard_map/ppermute | solution.py:334
  18.4 0.0 collective-permute-start.12
  18.4 0.0 collective-permute-done.9.refs_4_
  18.4 0.8 %collective-permute-start.4 = (bf16[64,1536]{1,0:T(8,128)(2,1)S(1)}, bf16[64,1536]{1,0:T(8,128)(2,1)S(1)}, u32[]{:S(2)}, u32[]{:S(2)}) collective-permute-start(bf16[64,1536]{1,0:T(8,128)(2,1)S(1)} %shard_map.39.refs_1_), channel_id=1, source_target_pairs={{0,1},{1,0},{2,3},{3,2},{4,5},{5,4},{6,7},{7,6},{8,9},{9,8},{10,11... | collective-permute-start | bytes 589832 | tf_op jit(solution)/shard_map/ppermute | solution.py:331
  19.2 0.0 collective-permute-done.10.refs_5_
  19.2 1.6 %collective-permute-start.5 = (bf16[64,1536]{1,0:T(8,128)(2,1)S(1)}, bf16[64,1536]{1,0:T(8,128)(2,1)S(1)}, u32[]{:S(2)}, u32[]{:S(2)}) collective-permute-start(bf16[64,1536]{1,0:T(8,128)(2,1)S(1)} %shard_map.39.refs_1_), channel_id=1, source_target_pairs={{0,2},{1,3},{2,0},{3,1},{4,6},{5,7},{6,4},{7,5},{8,10},{9,11},{10,... | collective-permute-start | bytes 589832 | tf_op jit(solution)/shard_map/ppermute | solution.py:334
  20.7 2.4 %shard_map.41 = (bf16[2048,1024]{1,0:T(8,128)(2,1)S(1)}, bf16[2048,2048]{1,0:T(8,128)(2,1)S(1)}, f32[2048,256]{1,0:T(8,128)S(1)}, bf16[2048,256]{1,0:T(8,128)(2,1)S(1)}, f32[8,128]{1,0:T(8,128)S(1)}) custom-call(bf16[64,1536]{1,0:T(8,128)(2,1)S(1)} %shard_map.40.refs_0_, ...), custom_call_target="tpu_custom_call", output_to_operand_aliasing={{0}: (8, {}), {1}: (9, {}), {2}: (10, {}), {3}: (11, {})} | custom-call | tf_op jit(solution)/shard_map/pallas_call | solution.py:340
  23.2 0.7 %collective-permute-done.14.refs_0_ = bf16[128,1536]{1,0:T(8,128)(2,1)S(1)} collective-permute-done((bf16[128,1536]{1,0:T(8,128)(2,1)S(1)}, bf16[128,1536]{1,0:T(8,128)(2,1)S(1)}, u32[]{:S(2)}, u32[]{:S(2)}) %collective-permute-start.14) | collective-permute-done | bytes 393248 | tf_op jit(solution)/shard_map/ppermute | solution.py:328
  23.9 0.0 collective-permute-start.15
  23.9 1.8 %collective-permute-done.4.refs_0_ = bf16[64,1536]{1,0:T(8,128)(2,1)S(1)} collective-permute-done((bf16[64,1536]{1,0:T(8,128)(2,1)S(1)}, bf16[64,1536]{1,0:T(8,128)(2,1)S(1)}, u32[]{:S(2)}, u32[]{:S(2)}) %collective-permute-start.4) | collective-permute-done | bytes 196640 | tf_op jit(solution)/shard_map/ppermute | solution.py:331
  25.7 0.2 collective-permute-done.5.refs_1_
  25.9 0.1 collective-permute-start.13
  26.0 0.0 collective-permute-done.15.refs_1_
  26.0 2.3 %shard_map.44 = (bf16[2048,1024]{1,0:T(8,128)(2,1)S(1)}, bf16[2048,2048]{1,0:T(8,128)(2,1)S(1)}, f32[2048,256]{1,0:T(8,128)S(1)}, bf16[2048,256]{1,0:T(8,128)(2,1)S(1)}, f32[8,128]{1,0:T(8,128)}) custom-call(bf16[128,1536]{1,0:T(8,128)(2,1)S(1)} %shard_map.43.refs_0_, ...), custom_call_target="tpu_custom_call", output_to_operand_aliasing={{0}: (2, {}), {1}: (3, {}), {2}: (4, {}), {3}: (5, {})} | custom-call | tf_op jit(solution)/shard_map/pallas_call | solution.py:340
  28.3 17.3 %shard_map.45 = f32[64,256]{1,0:T(8,128)} custom-call(bf16[128,1536]{1,0:T(8,128)(2,1)S(1)} %shard_map.42.refs_0_, bf16[128,1536]{1,0:T(8,128)(2,1)S(1)} %collective-permute-done.13.refs_1_, bf16[2048,1024]{1,0:T(8,128)(2,1)S(1)} %get-tuple-element.37.refs_2_, bf16[2048,2048]{1,0:T(8,128)(2,1)S(1)} %get-tuple-element.38.refs_3_, ...), custom_call_target="tpu_custom_call" | custom-call | tf_op jit(solution)/shard_map/pallas_call | solution.py:386
  (9 shorter events, 0.0 us)
Async XLA Ops:
  0.0 4.9 %collective-permute-start.1 = (bf16[2,512,256]{2,1,0:T(8,128)(2,1)}, bf16[2,512,256]{2,1,0:T(8,128)(2,1)S(1)}, u32[]{:S(2)}, u32[]{:S(2)}) collective-permute-start(bf16[2,512,256]{2,1,0:T(8,128)(2,1)} %refs_0_.1), channel_id=1, source_target_pairs={{0,8},{8,0},{16,24},{24,16},{1,9},{9,1},{17,25},{25,17},{2,10},{10... | collective-permute-start | bytes 1572872 | tf_op jit(solution)/shard_map/ppermute | solution.py:325
  0.5 4.4 %collective-permute-start.2 = (bf16[2,512,256]{2,1,0:T(8,128)(2,1)}, bf16[2,512,256]{2,1,0:T(8,128)(2,1)S(1)}, u32[]{:S(2)}, u32[]{:S(2)}) collective-permute-start(bf16[2,512,256]{2,1,0:T(8,128)(2,1)} %refs_1_.1), channel_id=1, source_target_pairs={{0,8},{8,0},{16,24},{24,16},{1,9},{9,1},{17,25},{25,17},{2,10},{10... | collective-permute-start | bytes 1572872 | tf_op jit(solution)/shard_map/ppermute | solution.py:325
  0.5 4.4 %collective-permute-start.3 = (f32[512,256]{1,0:T(8,128)}, f32[512,256]{1,0:T(8,128)S(1)}, u32[]{:S(2)}, u32[]{:S(2)}) collective-permute-start(f32[512,256]{1,0:T(8,128)} %refs_2_.1), channel_id=1, source_target_pairs={{0,8},{8,0},{16,24},{24,16},{1,9},{9,1},{17,25},{25,17},{2,10},{10... | collective-permute-start | bytes 1572872 | tf_op jit(solution)/shard_map/ppermute | solution.py:325
  2.2 8.3 %collective-permute-start.6 = (bf16[64,1536]{1,0:T(8,128)(2,1)S(1)}, bf16[64,1536]{1,0:T(8,128)(2,1)S(1)}, u32[]{:S(2)}, u32[]{:S(2)}) collective-permute-start(bf16[64,1536]{1,0:T(8,128)(2,1)S(1)} %get-tuple-element.26), channel_id=1, source_target_pairs={{0,16},{8,24},{16,0},{24,8},{1,17},{9,25},{17,1},{25,9},{2,18},{10... | collective-permute-start | bytes 589832 | tf_op jit(solution)/shard_map/ppermute | solution.py:328
  4.8 10.8 %collective-permute-start = (bf16[64,1536]{1,0:T(8,128)(2,1)S(1)}, bf16[64,1536]{1,0:T(8,128)(2,1)S(1)}, u32[]{:S(2)}, u32[]{:S(2)}) collective-permute-start(bf16[64,1536]{1,0:T(8,128)(2,1)S(1)} %get-tuple-element.23), channel_id=1, source_target_pairs={{0,16},{8,24},{16,0},{24,8},{1,17},{9,25},{17,1},{25,9},{2,18},{10... | collective-permute-start | bytes 589832 | tf_op jit(solution)/shard_map/ppermute | solution.py:328
  10.6 6.6 %collective-permute-start.7 = (bf16[64,1536]{1,0:T(8,128)(2,1)S(1)}, bf16[64,1536]{1,0:T(8,128)(2,1)S(1)}, u32[]{:S(2)}, u32[]{:S(2)}) collective-permute-start(bf16[64,1536]{1,0:T(8,128)(2,1)S(1)} %shard_map.40.refs_0_), channel_id=1, source_target_pairs={{0,1},{1,0},{2,3},{3,2},{4,5},{5,4},{6,7},{7,6},{8,9},{9,8},{10,11... | collective-permute-start | bytes 589832 | tf_op jit(solution)/shard_map/ppermute | solution.py:331
  12.5 5.9 %collective-permute-start.8 = (bf16[64,1536]{1,0:T(8,128)(2,1)S(1)}, bf16[64,1536]{1,0:T(8,128)(2,1)S(1)}, u32[]{:S(2)}, u32[]{:S(2)}) collective-permute-start(bf16[64,1536]{1,0:T(8,128)(2,1)S(1)} %shard_map.40.refs_0_), channel_id=1, source_target_pairs={{0,2},{1,3},{2,0},{3,1},{4,6},{5,7},{6,4},{7,5},{8,10},{9,11},{10,... | collective-permute-start | bytes 589832 | tf_op jit(solution)/shard_map/ppermute | solution.py:334
  14.1 9.8 %collective-permute-start.14 = (bf16[128,1536]{1,0:T(8,128)(2,1)S(1)}, bf16[128,1536]{1,0:T(8,128)(2,1)S(1)}, u32[]{:S(2)}, u32[]{:S(2)}) collective-permute-start(bf16[128,1536]{1,0:T(8,128)(2,1)S(1)} %get-tuple-element.32), channel_id=1, source_target_pairs={{0,16},{8,24},{16,0},{24,8},{1,17},{9,25},{17,1},{25,9},{2,18},{10... | collective-permute-start | bytes 1179656 | tf_op jit(solution)/shard_map/ppermute | solution.py:328
  15.6 2.8 %collective-permute-start.9 = (bf16[64,1536]{1,0:T(8,128)(2,1)S(1)}, bf16[64,1536]{1,0:T(8,128)(2,1)S(1)}, u32[]{:S(2)}, u32[]{:S(2)}) collective-permute-start(bf16[64,1536]{1,0:T(8,128)(2,1)S(1)} %shard_map.40.refs_0_), channel_id=1, source_target_pairs={{0,8},{8,0},{16,24},{24,16},{1,9},{9,1},{17,25},{25,17},{2,10},{10... | collective-permute-start | bytes 589832 | tf_op jit(solution)/shard_map/ppermute | solution.py:325
  15.6 3.6 %collective-permute-start.10 = (bf16[64,1536]{1,0:T(8,128)(2,1)S(1)}, bf16[64,1536]{1,0:T(8,128)(2,1)S(1)}, u32[]{:S(2)}, u32[]{:S(2)}) collective-permute-start(bf16[64,1536]{1,0:T(8,128)(2,1)S(1)} %shard_map.39.refs_1_), channel_id=1, source_target_pairs={{0,8},{8,0},{16,24},{24,16},{1,9},{9,1},{17,25},{25,17},{2,10},{10... | collective-permute-start | bytes 589832 | tf_op jit(solution)/shard_map/ppermute | solution.py:325
  17.1 3.6 %collective-permute-start.11 = (bf16[64,1536]{1,0:T(8,128)(2,1)S(1)}, bf16[64,1536]{1,0:T(8,128)(2,1)S(1)}, u32[]{:S(2)}, u32[]{:S(2)}) collective-permute-start(bf16[64,1536]{1,0:T(8,128)(2,1)S(1)} %collective-permute-done.7.refs_2_), channel_id=1, source_target_pairs={{0,8},{8,0},{16,24},{24,16},{1,9},{9,1},{17,25},{25,17},{2,10},{10... | collective-permute-start | bytes 589832 | tf_op jit(solution)/shard_map/ppermute | solution.py:325
  18.4 2.4 %collective-permute-start.12 = (bf16[64,1536]{1,0:T(8,128)(2,1)S(1)}, bf16[64,1536]{1,0:T(8,128)(2,1)S(1)}, u32[]{:S(2)}, u32[]{:S(2)}) collective-permute-start(bf16[64,1536]{1,0:T(8,128)(2,1)S(1)} %collective-permute-done.8.refs_3_), channel_id=1, source_target_pairs={{0,8},{8,0},{16,24},{24,16},{1,9},{9,1},{17,25},{25,17},{2,10},{10... | collective-permute-start | bytes 589832 | tf_op jit(solution)/shard_map/ppermute | solution.py:325
  18.4 7.3 %collective-permute-start.4 = (bf16[64,1536]{1,0:T(8,128)(2,1)S(1)}, bf16[64,1536]{1,0:T(8,128)(2,1)S(1)}, u32[]{:S(2)}, u32[]{:S(2)}) collective-permute-start(bf16[64,1536]{1,0:T(8,128)(2,1)S(1)} %shard_map.39.refs_1_), channel_id=1, source_target_pairs={{0,1},{1,0},{2,3},{3,2},{4,5},{5,4},{6,7},{7,6},{8,9},{9,8},{10,11... | collective-permute-start | bytes 589832 | tf_op jit(solution)/shard_map/ppermute | solution.py:331
  19.2 6.8 %collective-permute-start.5 = (bf16[64,1536]{1,0:T(8,128)(2,1)S(1)}, bf16[64,1536]{1,0:T(8,128)(2,1)S(1)}, u32[]{:S(2)}, u32[]{:S(2)}) collective-permute-start(bf16[64,1536]{1,0:T(8,128)(2,1)S(1)} %shard_map.39.refs_1_), channel_id=1, source_target_pairs={{0,2},{1,3},{2,0},{3,1},{4,6},{5,7},{6,4},{7,5},{8,10},{9,11},{10,... | collective-permute-start | bytes 589832 | tf_op jit(solution)/shard_map/ppermute | solution.py:334
  23.9 2.2 %collective-permute-start.15 = (bf16[128,1536]{1,0:T(8,128)(2,1)S(1)}, bf16[128,1536]{1,0:T(8,128)(2,1)S(1)}, u32[]{:S(2)}, u32[]{:S(2)}) collective-permute-start(bf16[128,1536]{1,0:T(8,128)(2,1)S(1)} %shard_map.43.refs_0_), channel_id=1, source_target_pairs={{0,8},{8,0},{16,24},{24,16},{1,9},{9,1},{17,25},{25,17},{2,10},{10... | collective-permute-start | bytes 1179656 | tf_op jit(solution)/shard_map/ppermute | solution.py:325
  25.9 2.4 %collective-permute-start.13 = (bf16[128,1536]{1,0:T(8,128)(2,1)S(1)}, bf16[128,1536]{1,0:T(8,128)(2,1)S(1)}, u32[]{:S(2)}, u32[]{:S(2)}) collective-permute-start(bf16[128,1536]{1,0:T(8,128)(2,1)S(1)} %shard_map.42.refs_0_), channel_id=1, source_target_pairs={{0,8},{8,0},{16,24},{24,16},{1,9},{9,1},{17,25},{25,17},{2,10},{10... | collective-permute-start | bytes 1179656 | tf_op jit(solution)/shard_map/ppermute | solution.py:325

commit v4 on v3

--- a/solution.py
+++ b/solution.py
@@ -128,12 +128,16 @@
     )(act, grad, targets)
 
 
+def tiles(low, high):
+    return [(at, min(at + TILE, high)) for at in range(low, high, TILE)]
+
+
 def build(layers, scale, low, high, data, kernel):
     width = data.shape[1] // (2 * layers)
-    for at in range(low, high, TILE):
-        cols = slice(at, at + TILE)
-        for row_at in range(0, at + TILE, TILE):
-            rows = slice(row_at, row_at + TILE)
+    for tile in tiles(low, high):
+        cols = slice(*tile)
+        for other in [*tiles(0, tile[0]), tile]:
+            rows = slice(*other)
             total = None
             for layer in range(layers):
                 a = slice(layer * width, (layer + 1) * width)
@@ -144,17 +148,16 @@
                 total = term if total is None else total + term
             block = (total * (1.0 / scale)).astype(jnp.bfloat16)
             kernel[rows, cols] = block
-            if row_at != at:
+            if other != tile:
                 kernel[cols, rows] = block.T
 
 
 def begin(low, high, kernel, residual, squashed):
-    for at in range(low, high, TILE):
-        cols = slice(at, at + TILE)
+    for tile in tiles(low, high):
+        cols = slice(*tile)
         squashed[cols, :] = jnp.tanh(residual[cols, :]).astype(jnp.bfloat16)
-    for at in range(0, high, TILE):
-        rows = slice(at, at + TILE)
-        cols = slice(low if at < low else 0, high)
+    for tile in tiles(0, low) + tiles(low, high):
+        rows, cols = slice(*tile), slice(low if tile[0] < low else 0, high)
         residual[rows, :] -= RATE * jnp.dot(
             kernel[rows, cols], squashed[cols, :], preferred_element_type=jnp.float32
         )
@@ -206,27 +209,28 @@
     token[...] = jnp.zeros_like(token)
 
 
-def stage_kernel(layers, scale, low, count, *refs):
+def stage_kernel(layers, scale, low, count, sums, *refs):
     pieces, state, token = refs[:count], refs[-5:-1], refs[-1]
     data, kernel, residual, squashed = state
     high = unpack_pieces(pieces, low, data, residual)
     build(layers, scale, low, high, data, kernel)
-    begin(low, high, kernel, residual, squashed)
+    if sums:
+        begin(low, high, kernel, residual, squashed)
     token[...] = jnp.zeros_like(token)
 
 
-def last_kernel(layers, scale, low, count, *refs):
+def last_kernel(layers, scale, start, low, count, *refs):
     pieces, state = refs[:count], refs[count : count + 4]
     result, other = refs[count + 4 :]
     data, kernel, residual, squashed = state
     share = result.shape[0]
     high = unpack_pieces(pieces, low, data, residual)
     build(layers, scale, low, high, data, kernel)
-    for at in range(low, high, TILE):
-        cols = slice(at, at + TILE)
+    for tile in tiles(start, high):
+        cols = slice(*tile)
         squashed[cols, :] = jnp.tanh(residual[cols, :]).astype(jnp.bfloat16)
-    for at in range(0, high, TILE):
-        rows, cols = slice(at, at + TILE), slice(low if at < low else 0, high)
+    for tile in tiles(0, start) + tiles(start, high):
+        rows, cols = slice(*tile), slice(start if tile[0] < start else 0, high)
         value = residual[rows, :] - RATE * jnp.dot(
             kernel[rows, cols], squashed[cols, :], preferred_element_type=jnp.float32
         )
@@ -235,8 +239,8 @@
     panels = (squashed, other)
     for step in range(1, ITERS - 1):
         now, later = panels[step % 2], panels[(step + 1) % 2]
-        for at in range(0, high, TILE):
-            rows = slice(at, at + TILE)
+        for at in range(0, high, 4 * TILE):
+            rows = slice(at, at + 4 * TILE)
             update = jnp.dot(
                 kernel[rows, :], now[...], preferred_element_type=jnp.float32
             )
@@ -335,16 +339,16 @@
 
     shapes = state_shapes(examples, 2 * layers * width, out)
 
-    def stage(state, low, pieces, *tokens):
+    def stage(state, low, pieces, sums=True):
         count = len(pieces)
         *state, token = pl.pallas_call(
-            functools.partial(stage_kernel, layers, scale, low, count),
+            functools.partial(stage_kernel, layers, scale, low, count, sums),
             out_shape=[*shapes, TOKEN],
-            in_specs=[IN_VMEM] * (count + 4) + [IN_HBM] * len(tokens),
+            in_specs=[IN_VMEM] * (count + 4),
             out_specs=[IN_VMEM] * 5,
             input_output_aliases={count + i: i for i in range(4)},
             compiler_params=PARAMS,
-        )(*pieces, *state, *tokens)
+        )(*pieces, *state)
         return state, token
 
     own = [
@@ -375,16 +379,16 @@
     low = 2 * rows
     four = [first, second, near_first, far_first]
     state, token = stage(state, low, four + [twin(piece) for piece in four])
-    low += 4 * quarter
+    low += 2 * sum(piece.shape[0] for piece in four)
     last = join([near_second, far_second], token)
     third = after(third, token)
-    state, token = stage(state, low, [third, twin(third)])
-    low += 2 * quarter
+    state, token = stage(state, low, [third, twin(third)], sums=False)
+    start, low = low, low + 2 * quarter
     pieces = last
     pieces = [pieces, twin(pieces)]
     count = len(pieces)
     return pl.pallas_call(
-        functools.partial(last_kernel, layers, scale, low, count),
+        functools.partial(last_kernel, layers, scale, start, low, count),
         out_shape=jax.ShapeDtypeStruct((share, out), jnp.float32),
         in_specs=[IN_VMEM] * (count + 4),
         out_specs=IN_VMEM,

time: 45.8 us -> 44.8 us (0.978)
  Pallas kernels: 26.8 us -> 25.8 us
    pallas_call x3, Pallas kernels: 22 us -> 21 us  [the longest x1 16.8 us: whole_body(): pl.pallas_call(functools.partial(last_kernel, layers, scale, start, low,...]
  transfers between devices with their start and end apart: 16 -> 16, of which waited for: 6 -> 6; matrix products, arithmetic and copies ran while one was open for 0% -> 0% of each run, Pallas kernels for 21% -> 20%
where the time goes in v4:
time: 44.8 us; the launch traced here: 44.6 us
  Pallas kernels  25.8 us (58%)
  starting transfers between devices  11.6 us (26%)
  waiting for transfers between devices  7.15 us (16%)
    pallas_call x1, Pallas kernels, whole_body(): pl.pallas_call(functools.partial(last_kernel, layers, scale, start, low,...  16.8 us
    pallas_call x2, Pallas kernels, stage(): pl.pallas_call(functools.partial(stage_kernel, layers, scale, low, count,...  4.19 us
    ppermute x3, starting transfers between devices, across(): return lax.ppermute(value, 'row', [(i, i ^ 2) for i in range(row_count)])  4.18 us
    pallas_call x1, Pallas kernels, whole_body(): pl.pallas_call(functools.partial(first_kernel, layers, scale), out_shape=...  3.5 us
    ppermute x2, starting transfers between devices, far(): return lax.ppermute(value, 'col', [(i, i ^ 2) for i in range(col_count)])  3.15 us
    ppermute x2, waiting for transfers between devices, near(): return lax.ppermute(value, 'col', [(i, i ^ 1) for i in range(col_count)])  2.83 us
    ppermute x3, waiting for transfers between devices, across(): return lax.ppermute(value, 'row', [(i, i ^ 2) for i in range(row_count)])  2.83 us
    ppermute x2, starting transfers between devices, near(): return lax.ppermute(value, 'col', [(i, i ^ 1) for i in range(col_count)])  2.71 us
  transfers between devices with their start and end apart: 16, of which 6 were waited for; matrix products, arithmetic and copies ran while one was open for 0% of the time, Pallas kernels for 20%

profile of v4, /device:TPU:0, one launch (start us, length us, event | category | flops | bytes accessed | tf_op | source)
XLA Modules:
  0.0 44.6 jit_solution(15622199355784107730)
XLA Ops:
  0.0 0.5 %collective-permute-start.1 = (bf16[2,512,256]{2,1,0:T(8,128)(2,1)}, bf16[2,512,256]{2,1,0:T(8,128)(2,1)S(1)}, u32[]{:S(2)}, u32[]{:S(2)}) collective-permute-start(bf16[2,512,256]{2,1,0:T(8,128)(2,1)} %refs_0_.1), channel_id=1, source_target_pairs={{0,8},{8,0},{16,24},{24,16},{1,9},{9,1},{17,25},{25,17},{2,10},{10... | collective-permute-start | bytes 1572872 | tf_op jit(solution)/shard_map/ppermute | solution.py:329
  0.5 0.1 collective-permute-start.2
  0.5 0.5 %collective-permute-start.3 = (f32[512,256]{1,0:T(8,128)}, f32[512,256]{1,0:T(8,128)S(1)}, u32[]{:S(2)}, u32[]{:S(2)}) collective-permute-start(f32[512,256]{1,0:T(8,128)} %refs_2_.1), channel_id=1, source_target_pairs={{0,8},{8,0},{16,24},{24,16},{1,9},{9,1},{17,25},{25,17},{2,10},{10... | collective-permute-start | bytes 1572872 | tf_op jit(solution)/shard_map/ppermute | solution.py:329
  1.0 1.3 %shard_map.37 = (bf16[64,1536]{1,0:T(8,128)(2,1)S(1)}, bf16[64,1536]{1,0:T(8,128)(2,1)S(1)}, bf16[128,1536]{1,0:T(8,128)(2,1)S(1)}, f32[8,128]{1,0:T(8,128)S(1)}) custom-call(bf16[2,512,256]{2,1,0:T(8,128)(2,1)} %refs_0_.1, bf16[2,512,256]{2,1,0:T(8,128)(2,1)} %refs_1_.1, f32[512,256]{1,0:T(8,128)} %refs_2_.1), custom_call_target="tpu_custom_call" | custom-call | tf_op jit(solution)/shard_map/pallas_call | solution.py:116
  2.2 2.6 %collective-permute-start.6 = (bf16[64,1536]{1,0:T(8,128)(2,1)S(1)}, bf16[64,1536]{1,0:T(8,128)(2,1)S(1)}, u32[]{:S(2)}, u32[]{:S(2)}) collective-permute-start(bf16[64,1536]{1,0:T(8,128)(2,1)S(1)} %get-tuple-element.26), channel_id=1, source_target_pairs={{0,16},{8,24},{16,0},{24,8},{1,17},{9,25},{17,1},{25,9},{2,18},{10... | collective-permute-start | bytes 589832 | tf_op jit(solution)/shard_map/ppermute | solution.py:332
  4.8 0.1 collective-permute-start
  4.9 0.0 collective-permute-done.1.refs_3_
  4.9 0.0 collective-permute-done.2.refs_4_
  4.9 0.0 collective-permute-done.3.refs_5_
  4.9 3.5 %shard_map.38 = (bf16[2048,1024]{1,0:T(8,128)(2,1)S(1)}, bf16[2048,2048]{1,0:T(8,128)(2,1)S(1)}, f32[2048,256]{1,0:T(8,128)S(1)}, bf16[2048,256]{1,0:T(8,128)(2,1)S(1)}, f32[8,128]{1,0:T(8,128)S(1)}) custom-call(bf16[2,512,256]{2,1,0:T(8,128)(2,1)} %refs_0_.1, bf16[2,512,256]{2,1,0:T(8,128)(2,1)} %refs_1_.1, f32[512,256]{1,0:T(8,128)} %refs_2_.1, ...), custom_call_target="tpu_custom_call" | custom-call | flops 1610612736 | bytes 1048576 | tf_op jit(solution)/shard_map/pallas_call | solution.py:366
  8.4 2.2 %collective-permute-done.6.refs_0_ = bf16[64,1536]{1,0:T(8,128)(2,1)S(1)} collective-permute-done((bf16[64,1536]{1,0:T(8,128)(2,1)S(1)}, bf16[64,1536]{1,0:T(8,128)(2,1)S(1)}, u32[]{:S(2)}, u32[]{:S(2)}) %collective-permute-start.6) | collective-permute-done | bytes 196640 | tf_op jit(solution)/shard_map/ppermute | solution.py:332
  10.6 1.9 %collective-permute-start.7 = (bf16[64,1536]{1,0:T(8,128)(2,1)S(1)}, bf16[64,1536]{1,0:T(8,128)(2,1)S(1)}, u32[]{:S(2)}, u32[]{:S(2)}) collective-permute-start(bf16[64,1536]{1,0:T(8,128)(2,1)S(1)} %shard_map.40.refs_0_), channel_id=1, source_target_pairs={{0,1},{1,0},{2,3},{3,2},{4,5},{5,4},{6,7},{7,6},{8,9},{9,8},{10,11... | collective-permute-start | bytes 589832 | tf_op jit(solution)/shard_map/ppermute | solution.py:335
  12.5 1.6 %collective-permute-start.8 = (bf16[64,1536]{1,0:T(8,128)(2,1)S(1)}, bf16[64,1536]{1,0:T(8,128)(2,1)S(1)}, u32[]{:S(2)}, u32[]{:S(2)}) collective-permute-start(bf16[64,1536]{1,0:T(8,128)(2,1)S(1)} %shard_map.40.refs_0_), channel_id=1, source_target_pairs={{0,2},{1,3},{2,0},{3,1},{4,6},{5,7},{6,4},{7,5},{8,10},{9,11},{10,... | collective-permute-start | bytes 589832 | tf_op jit(solution)/shard_map/ppermute | solution.py:338
  14.1 1.5 %collective-permute-start.14 = (bf16[128,1536]{1,0:T(8,128)(2,1)S(1)}, bf16[128,1536]{1,0:T(8,128)(2,1)S(1)}, u32[]{:S(2)}, u32[]{:S(2)}) collective-permute-start(bf16[128,1536]{1,0:T(8,128)(2,1)S(1)} %get-tuple-element.32), channel_id=1, source_target_pairs={{0,16},{8,24},{16,0},{24,8},{1,17},{9,25},{17,1},{25,9},{2,18},{10... | collective-permute-start | bytes 1179656 | tf_op jit(solution)/shard_map/ppermute | solution.py:332
  15.6 0.0 collective-permute-start.9
  15.6 0.5 %collective-permute-start.10 = (bf16[64,1536]{1,0:T(8,128)(2,1)S(1)}, bf16[64,1536]{1,0:T(8,128)(2,1)S(1)}, u32[]{:S(2)}, u32[]{:S(2)}) collective-permute-start(bf16[64,1536]{1,0:T(8,128)(2,1)S(1)} %shard_map.39.refs_1_), channel_id=1, source_target_pairs={{0,8},{8,0},{16,24},{24,16},{1,9},{9,1},{17,25},{25,17},{2,10},{10... | collective-permute-start | bytes 589832 | tf_op jit(solution)/shard_map/ppermute | solution.py:329
  16.1 1.0 %collective-permute-done.7.refs_2_ = bf16[64,1536]{1,0:T(8,128)(2,1)S(1)} collective-permute-done((bf16[64,1536]{1,0:T(8,128)(2,1)S(1)}, bf16[64,1536]{1,0:T(8,128)(2,1)S(1)}, u32[]{:S(2)}, u32[]{:S(2)}) %collective-permute-start.7) | collective-permute-done | bytes 196640 | tf_op jit(solution)/shard_map/ppermute | solution.py:335
  17.1 1.2 %collective-permute-done.8.refs_3_ = bf16[64,1536]{1,0:T(8,128)(2,1)S(1)} collective-permute-done((bf16[64,1536]{1,0:T(8,128)(2,1)S(1)}, bf16[64,1536]{1,0:T(8,128)(2,1)S(1)}, u32[]{:S(2)}, u32[]{:S(2)}) %collective-permute-start.8) | collective-permute-done | bytes 196640 | tf_op jit(solution)/shard_map/ppermute | solution.py:338
  18.4 0.0 collective-permute-start.12
  18.4 0.0 collective-permute-done.9.refs_4_
  18.4 0.8 %collective-permute-start.4 = (bf16[64,1536]{1,0:T(8,128)(2,1)S(1)}, bf16[64,1536]{1,0:T(8,128)(2,1)S(1)}, u32[]{:S(2)}, u32[]{:S(2)}) collective-permute-start(bf16[64,1536]{1,0:T(8,128)(2,1)S(1)} %shard_map.39.refs_1_), channel_id=1, source_target_pairs={{0,1},{1,0},{2,3},{3,2},{4,5},{5,4},{6,7},{7,6},{8,9},{9,8},{10,11... | collective-permute-start | bytes 589832 | tf_op jit(solution)/shard_map/ppermute | solution.py:335
  19.2 0.0 collective-permute-done.10.refs_5_
  19.2 1.6 %collective-permute-start.5 = (bf16[64,1536]{1,0:T(8,128)(2,1)S(1)}, bf16[64,1536]{1,0:T(8,128)(2,1)S(1)}, u32[]{:S(2)}, u32[]{:S(2)}) collective-permute-start(bf16[64,1536]{1,0:T(8,128)(2,1)S(1)} %shard_map.39.refs_1_), channel_id=1, source_target_pairs={{0,2},{1,3},{2,0},{3,1},{4,6},{5,7},{6,4},{7,5},{8,10},{9,11},{10,... | collective-permute-start | bytes 589832 | tf_op jit(solution)/shard_map/ppermute | solution.py:338
  20.7 2.4 %shard_map.41 = (bf16[2048,1024]{1,0:T(8,128)(2,1)S(1)}, bf16[2048,2048]{1,0:T(8,128)(2,1)S(1)}, f32[2048,256]{1,0:T(8,128)S(1)}, bf16[2048,256]{1,0:T(8,128)(2,1)S(1)}, f32[8,128]{1,0:T(8,128)S(1)}) custom-call(bf16[64,1536]{1,0:T(8,128)(2,1)S(1)} %shard_map.40.refs_0_, ...), custom_call_target="tpu_custom_call", output_to_operand_aliasing={{0}: (8, {}), {1}: (9, {}), {2}: (10, {}), {3}: (11, {})} | custom-call | tf_op jit(solution)/shard_map/pallas_call | solution.py:344
  23.2 0.7 %collective-permute-done.14.refs_0_ = bf16[128,1536]{1,0:T(8,128)(2,1)S(1)} collective-permute-done((bf16[128,1536]{1,0:T(8,128)(2,1)S(1)}, bf16[128,1536]{1,0:T(8,128)(2,1)S(1)}, u32[]{:S(2)}, u32[]{:S(2)}) %collective-permute-start.14) | collective-permute-done | bytes 393248 | tf_op jit(solution)/shard_map/ppermute | solution.py:332
  23.9 0.0 collective-permute-start.15
  23.9 1.8 %collective-permute-done.4.refs_0_ = bf16[64,1536]{1,0:T(8,128)(2,1)S(1)} collective-permute-done((bf16[64,1536]{1,0:T(8,128)(2,1)S(1)}, bf16[64,1536]{1,0:T(8,128)(2,1)S(1)}, u32[]{:S(2)}, u32[]{:S(2)}) %collective-permute-start.4) | collective-permute-done | bytes 196640 | tf_op jit(solution)/shard_map/ppermute | solution.py:335
  25.7 0.2 collective-permute-done.5.refs_1_
  25.9 0.1 collective-permute-start.13
  26.0 0.0 collective-permute-done.15.refs_1_
  26.0 1.8 %shard_map.44 = (bf16[2048,1024]{1,0:T(8,128)(2,1)S(1)}, bf16[2048,2048]{1,0:T(8,128)(2,1)S(1)}, f32[2048,256]{1,0:T(8,128)S(1)}, bf16[2048,256]{1,0:T(8,128)(2,1)S(1)}, f32[8,128]{1,0:T(8,128)}) custom-call(bf16[128,1536]{1,0:T(8,128)(2,1)S(1)} %shard_map.43.refs_0_, ...), custom_call_target="tpu_custom_call", output_to_operand_aliasing={{0}: (2, {}), {1}: (3, {}), {2}: (4, {}), {3}: (5, {})} | custom-call | tf_op jit(solution)/shard_map/pallas_call | solution.py:344
  27.8 16.8 %shard_map.45 = f32[64,256]{1,0:T(8,128)} custom-call(bf16[128,1536]{1,0:T(8,128)(2,1)S(1)} %shard_map.42.refs_0_, bf16[128,1536]{1,0:T(8,128)(2,1)S(1)} %collective-permute-done.13.refs_1_, bf16[2048,1024]{1,0:T(8,128)(2,1)S(1)} %get-tuple-element.37.refs_2_, bf16[2048,2048]{1,0:T(8,128)(2,1)S(1)} %get-tuple-element.38.refs_3_, ...), custom_call_target="tpu_custom_call" | custom-call | tf_op jit(solution)/shard_map/pallas_call | solution.py:390
  (9 shorter events, 0.0 us)
Async XLA Ops:
  0.0 4.9 %collective-permute-start.1 = (bf16[2,512,256]{2,1,0:T(8,128)(2,1)}, bf16[2,512,256]{2,1,0:T(8,128)(2,1)S(1)}, u32[]{:S(2)}, u32[]{:S(2)}) collective-permute-start(bf16[2,512,256]{2,1,0:T(8,128)(2,1)} %refs_0_.1), channel_id=1, source_target_pairs={{0,8},{8,0},{16,24},{24,16},{1,9},{9,1},{17,25},{25,17},{2,10},{10... | collective-permute-start | bytes 1572872 | tf_op jit(solution)/shard_map/ppermute | solution.py:329
  0.5 4.4 %collective-permute-start.2 = (bf16[2,512,256]{2,1,0:T(8,128)(2,1)}, bf16[2,512,256]{2,1,0:T(8,128)(2,1)S(1)}, u32[]{:S(2)}, u32[]{:S(2)}) collective-permute-start(bf16[2,512,256]{2,1,0:T(8,128)(2,1)} %refs_1_.1), channel_id=1, source_target_pairs={{0,8},{8,0},{16,24},{24,16},{1,9},{9,1},{17,25},{25,17},{2,10},{10... | collective-permute-start | bytes 1572872 | tf_op jit(solution)/shard_map/ppermute | solution.py:329
  0.5 4.4 %collective-permute-start.3 = (f32[512,256]{1,0:T(8,128)}, f32[512,256]{1,0:T(8,128)S(1)}, u32[]{:S(2)}, u32[]{:S(2)}) collective-permute-start(f32[512,256]{1,0:T(8,128)} %refs_2_.1), channel_id=1, source_target_pairs={{0,8},{8,0},{16,24},{24,16},{1,9},{9,1},{17,25},{25,17},{2,10},{10... | collective-permute-start | bytes 1572872 | tf_op jit(solution)/shard_map/ppermute | solution.py:329
  2.2 8.3 %collective-permute-start.6 = (bf16[64,1536]{1,0:T(8,128)(2,1)S(1)}, bf16[64,1536]{1,0:T(8,128)(2,1)S(1)}, u32[]{:S(2)}, u32[]{:S(2)}) collective-permute-start(bf16[64,1536]{1,0:T(8,128)(2,1)S(1)} %get-tuple-element.26), channel_id=1, source_target_pairs={{0,16},{8,24},{16,0},{24,8},{1,17},{9,25},{17,1},{25,9},{2,18},{10... | collective-permute-start | bytes 589832 | tf_op jit(solution)/shard_map/ppermute | solution.py:332
  4.8 10.8 %collective-permute-start = (bf16[64,1536]{1,0:T(8,128)(2,1)S(1)}, bf16[64,1536]{1,0:T(8,128)(2,1)S(1)}, u32[]{:S(2)}, u32[]{:S(2)}) collective-permute-start(bf16[64,1536]{1,0:T(8,128)(2,1)S(1)} %get-tuple-element.23), channel_id=1, source_target_pairs={{0,16},{8,24},{16,0},{24,8},{1,17},{9,25},{17,1},{25,9},{2,18},{10... | collective-permute-start | bytes 589832 | tf_op jit(solution)/shard_map/ppermute | solution.py:332
  10.6 6.6 %collective-permute-start.7 = (bf16[64,1536]{1,0:T(8,128)(2,1)S(1)}, bf16[64,1536]{1,0:T(8,128)(2,1)S(1)}, u32[]{:S(2)}, u32[]{:S(2)}) collective-permute-start(bf16[64,1536]{1,0:T(8,128)(2,1)S(1)} %shard_map.40.refs_0_), channel_id=1, source_target_pairs={{0,1},{1,0},{2,3},{3,2},{4,5},{5,4},{6,7},{7,6},{8,9},{9,8},{10,11... | collective-permute-start | bytes 589832 | tf_op jit(solution)/shard_map/ppermute | solution.py:335
  12.5 5.9 %collective-permute-start.8 = (bf16[64,1536]{1,0:T(8,128)(2,1)S(1)}, bf16[64,1536]{1,0:T(8,128)(2,1)S(1)}, u32[]{:S(2)}, u32[]{:S(2)}) collective-permute-start(bf16[64,1536]{1,0:T(8,128)(2,1)S(1)} %shard_map.40.refs_0_), channel_id=1, source_target_pairs={{0,2},{1,3},{2,0},{3,1},{4,6},{5,7},{6,4},{7,5},{8,10},{9,11},{10,... | collective-permute-start | bytes 589832 | tf_op jit(solution)/shard_map/ppermute | solution.py:338
  14.1 9.8 %collective-permute-start.14 = (bf16[128,1536]{1,0:T(8,128)(2,1)S(1)}, bf16[128,1536]{1,0:T(8,128)(2,1)S(1)}, u32[]{:S(2)}, u32[]{:S(2)}) collective-permute-start(bf16[128,1536]{1,0:T(8,128)(2,1)S(1)} %get-tuple-element.32), channel_id=1, source_target_pairs={{0,16},{8,24},{16,0},{24,8},{1,17},{9,25},{17,1},{25,9},{2,18},{10... | collective-permute-start | bytes 1179656 | tf_op jit(solution)/shard_map/ppermute | solution.py:332
  15.6 2.8 %collective-permute-start.9 = (bf16[64,1536]{1,0:T(8,128)(2,1)S(1)}, bf16[64,1536]{1,0:T(8,128)(2,1)S(1)}, u32[]{:S(2)}, u32[]{:S(2)}) collective-permute-start(bf16[64,1536]{1,0:T(8,128)(2,1)S(1)} %shard_map.40.refs_0_), channel_id=1, source_target_pairs={{0,8},{8,0},{16,24},{24,16},{1,9},{9,1},{17,25},{25,17},{2,10},{10... | collective-permute-start | bytes 589832 | tf_op jit(solution)/shard_map/ppermute | solution.py:329
  15.6 3.6 %collective-permute-start.10 = (bf16[64,1536]{1,0:T(8,128)(2,1)S(1)}, bf16[64,1536]{1,0:T(8,128)(2,1)S(1)}, u32[]{:S(2)}, u32[]{:S(2)}) collective-permute-start(bf16[64,1536]{1,0:T(8,128)(2,1)S(1)} %shard_map.39.refs_1_), channel_id=1, source_target_pairs={{0,8},{8,0},{16,24},{24,16},{1,9},{9,1},{17,25},{25,17},{2,10},{10... | collective-permute-start | bytes 589832 | tf_op jit(solution)/shard_map/ppermute | solution.py:329
  17.1 3.6 %collective-permute-start.11 = (bf16[64,1536]{1,0:T(8,128)(2,1)S(1)}, bf16[64,1536]{1,0:T(8,128)(2,1)S(1)}, u32[]{:S(2)}, u32[]{:S(2)}) collective-permute-start(bf16[64,1536]{1,0:T(8,128)(2,1)S(1)} %collective-permute-done.7.refs_2_), channel_id=1, source_target_pairs={{0,8},{8,0},{16,24},{24,16},{1,9},{9,1},{17,25},{25,17},{2,10},{10... | collective-permute-start | bytes 589832 | tf_op jit(solution)/shard_map/ppermute | solution.py:329
  18.4 2.4 %collective-permute-start.12 = (bf16[64,1536]{1,0:T(8,128)(2,1)S(1)}, bf16[64,1536]{1,0:T(8,128)(2,1)S(1)}, u32[]{:S(2)}, u32[]{:S(2)}) collective-permute-start(bf16[64,1536]{1,0:T(8,128)(2,1)S(1)} %collective-permute-done.8.refs_3_), channel_id=1, source_target_pairs={{0,8},{8,0},{16,24},{24,16},{1,9},{9,1},{17,25},{25,17},{2,10},{10... | collective-permute-start | bytes 589832 | tf_op jit(solution)/shard_map/ppermute | solution.py:329
  18.4 7.3 %collective-permute-start.4 = (bf16[64,1536]{1,0:T(8,128)(2,1)S(1)}, bf16[64,1536]{1,0:T(8,128)(2,1)S(1)}, u32[]{:S(2)}, u32[]{:S(2)}) collective-permute-start(bf16[64,1536]{1,0:T(8,128)(2,1)S(1)} %shard_map.39.refs_1_), channel_id=1, source_target_pairs={{0,1},{1,0},{2,3},{3,2},{4,5},{5,4},{6,7},{7,6},{8,9},{9,8},{10,11... | collective-permute-start | bytes 589832 | tf_op jit(solution)/shard_map/ppermute | solution.py:335
  19.2 6.8 %collective-permute-start.5 = (bf16[64,1536]{1,0:T(8,128)(2,1)S(1)}, bf16[64,1536]{1,0:T(8,128)(2,1)S(1)}, u32[]{:S(2)}, u32[]{:S(2)}) collective-permute-start(bf16[64,1536]{1,0:T(8,128)(2,1)S(1)} %shard_map.39.refs_1_), channel_id=1, source_target_pairs={{0,2},{1,3},{2,0},{3,1},{4,6},{5,7},{6,4},{7,5},{8,10},{9,11},{10,... | collective-permute-start | bytes 589832 | tf_op jit(solution)/shard_map/ppermute | solution.py:338
  23.9 2.2 %collective-permute-start.15 = (bf16[128,1536]{1,0:T(8,128)(2,1)S(1)}, bf16[128,1536]{1,0:T(8,128)(2,1)S(1)}, u32[]{:S(2)}, u32[]{:S(2)}) collective-permute-start(bf16[128,1536]{1,0:T(8,128)(2,1)S(1)} %shard_map.43.refs_0_), channel_id=1, source_target_pairs={{0,8},{8,0},{16,24},{24,16},{1,9},{9,1},{17,25},{25,17},{2,10},{10... | collective-permute-start | bytes 1179656 | tf_op jit(solution)/shard_map/ppermute | solution.py:329
  25.9 1.8 %collective-permute-start.13 = (bf16[128,1536]{1,0:T(8,128)(2,1)S(1)}, bf16[128,1536]{1,0:T(8,128)(2,1)S(1)}, u32[]{:S(2)}, u32[]{:S(2)}) collective-permute-start(bf16[128,1536]{1,0:T(8,128)(2,1)S(1)} %shard_map.42.refs_0_), channel_id=1, source_target_pairs={{0,8},{8,0},{16,24},{24,16},{1,9},{9,1},{17,25},{25,17},{2,10},{10... | collective-permute-start | bytes 1179656 | tf_op jit(solution)/shard_map/ppermute | solution.py:329

commit v5 on v4

--- a/solution.py
+++ b/solution.py
@@ -128,8 +128,8 @@
     )(act, grad, targets)
 
 
-def tiles(low, high):
-    return [(at, min(at + TILE, high)) for at in range(low, high, TILE)]
+def tiles(low, high, size=TILE):
+    return [(at, min(at + size, high)) for at in range(low, high, size)]
 
 
 def build(layers, scale, low, high, data, kernel):
@@ -229,7 +229,7 @@
     for tile in tiles(start, high):
         cols = slice(*tile)
         squashed[cols, :] = jnp.tanh(residual[cols, :]).astype(jnp.bfloat16)
-    for tile in tiles(0, start) + tiles(start, high):
+    for tile in tiles(0, start, 4 * TILE) + tiles(start, high, 4 * TILE):
         rows, cols = slice(*tile), slice(start if tile[0] < start else 0, high)
         value = residual[rows, :] - RATE * jnp.dot(
             kernel[rows, cols], squashed[cols, :], preferred_element_type=jnp.float32

time: 44.8 us -> 44.7 us (level)
  no operation moved by 1% of the time
where the time goes in v5:
time: 44.7 us; the launch traced here: 44.5 us
  Pallas kernels  25.7 us (57%)
  starting transfers between devices  11.6 us (26%)
  waiting for transfers between devices  7.15 us (16%)
    pallas_call x1, Pallas kernels, whole_body(): pl.pallas_call(functools.partial(last_kernel, layers, scale, start, low,...  16.7 us
    pallas_call x2, Pallas kernels, stage(): pl.pallas_call(functools.partial(stage_kernel, layers, scale, low, count,...  4.19 us
    ppermute x3, starting transfers between devices, across(): return lax.ppermute(value, 'row', [(i, i ^ 2) for i in range(row_count)])  4.18 us
    pallas_call x1, Pallas kernels, whole_body(): pl.pallas_call(functools.partial(first_kernel, layers, scale), out_shape=...  3.5 us
    ppermute x2, starting transfers between devices, far(): return lax.ppermute(value, 'col', [(i, i ^ 2) for i in range(col_count)])  3.15 us
    ppermute x2, waiting for transfers between devices, near(): return lax.ppermute(value, 'col', [(i, i ^ 1) for i in range(col_count)])  2.83 us
    ppermute x3, waiting for transfers between devices, across(): return lax.ppermute(value, 'row', [(i, i ^ 2) for i in range(row_count)])  2.83 us
    ppermute x2, starting transfers between devices, near(): return lax.ppermute(value, 'col', [(i, i ^ 1) for i in range(col_count)])  2.71 us
  transfers between devices with their start and end apart: 16, of which 6 were waited for; matrix products, arithmetic and copies ran while one was open for 0% of the time, Pallas kernels for 20%

profile of v5, /device:TPU:0, one launch (start us, length us, event | category | flops | bytes accessed | tf_op | source)
XLA Modules:
  0.0 44.5 jit_solution(7790383473004741683)
XLA Ops:
  0.0 0.5 %collective-permute-start.1 = (bf16[2,512,256]{2,1,0:T(8,128)(2,1)}, bf16[2,512,256]{2,1,0:T(8,128)(2,1)S(1)}, u32[]{:S(2)}, u32[]{:S(2)}) collective-permute-start(bf16[2,512,256]{2,1,0:T(8,128)(2,1)} %refs_0_.1), channel_id=1, source_target_pairs={{0,8},{8,0},{16,24},{24,16},{1,9},{9,1},{17,25},{25,17},{2,10},{10... | collective-permute-start | bytes 1572872 | tf_op jit(solution)/shard_map/ppermute | solution.py:329
  0.5 0.1 collective-permute-start.2
  0.5 0.5 %collective-permute-start.3 = (f32[512,256]{1,0:T(8,128)}, f32[512,256]{1,0:T(8,128)S(1)}, u32[]{:S(2)}, u32[]{:S(2)}) collective-permute-start(f32[512,256]{1,0:T(8,128)} %refs_2_.1), channel_id=1, source_target_pairs={{0,8},{8,0},{16,24},{24,16},{1,9},{9,1},{17,25},{25,17},{2,10},{10... | collective-permute-start | bytes 1572872 | tf_op jit(solution)/shard_map/ppermute | solution.py:329
  1.0 1.3 %shard_map.37 = (bf16[64,1536]{1,0:T(8,128)(2,1)S(1)}, bf16[64,1536]{1,0:T(8,128)(2,1)S(1)}, bf16[128,1536]{1,0:T(8,128)(2,1)S(1)}, f32[8,128]{1,0:T(8,128)S(1)}) custom-call(bf16[2,512,256]{2,1,0:T(8,128)(2,1)} %refs_0_.1, bf16[2,512,256]{2,1,0:T(8,128)(2,1)} %refs_1_.1, f32[512,256]{1,0:T(8,128)} %refs_2_.1), custom_call_target="tpu_custom_call" | custom-call | tf_op jit(solution)/shard_map/pallas_call | solution.py:116
  2.2 2.6 %collective-permute-start.6 = (bf16[64,1536]{1,0:T(8,128)(2,1)S(1)}, bf16[64,1536]{1,0:T(8,128)(2,1)S(1)}, u32[]{:S(2)}, u32[]{:S(2)}) collective-permute-start(bf16[64,1536]{1,0:T(8,128)(2,1)S(1)} %get-tuple-element.26), channel_id=1, source_target_pairs={{0,16},{8,24},{16,0},{24,8},{1,17},{9,25},{17,1},{25,9},{2,18},{10... | collective-permute-start | bytes 589832 | tf_op jit(solution)/shard_map/ppermute | solution.py:332
  4.8 0.1 collective-permute-start
  4.9 0.0 collective-permute-done.1.refs_3_
  4.9 0.0 collective-permute-done.2.refs_4_
  4.9 0.0 collective-permute-done.3.refs_5_
  4.9 3.5 %shard_map.38 = (bf16[2048,1024]{1,0:T(8,128)(2,1)S(1)}, bf16[2048,2048]{1,0:T(8,128)(2,1)S(1)}, f32[2048,256]{1,0:T(8,128)S(1)}, bf16[2048,256]{1,0:T(8,128)(2,1)S(1)}, f32[8,128]{1,0:T(8,128)S(1)}) custom-call(bf16[2,512,256]{2,1,0:T(8,128)(2,1)} %refs_0_.1, bf16[2,512,256]{2,1,0:T(8,128)(2,1)} %refs_1_.1, f32[512,256]{1,0:T(8,128)} %refs_2_.1, ...), custom_call_target="tpu_custom_call" | custom-call | flops 1610612736 | bytes 1048576 | tf_op jit(solution)/shard_map/pallas_call | solution.py:366
  8.4 2.2 %collective-permute-done.6.refs_0_ = bf16[64,1536]{1,0:T(8,128)(2,1)S(1)} collective-permute-done((bf16[64,1536]{1,0:T(8,128)(2,1)S(1)}, bf16[64,1536]{1,0:T(8,128)(2,1)S(1)}, u32[]{:S(2)}, u32[]{:S(2)}) %collective-permute-start.6) | collective-permute-done | bytes 196640 | tf_op jit(solution)/shard_map/ppermute | solution.py:332
  10.6 1.9 %collective-permute-start.7 = (bf16[64,1536]{1,0:T(8,128)(2,1)S(1)}, bf16[64,1536]{1,0:T(8,128)(2,1)S(1)}, u32[]{:S(2)}, u32[]{:S(2)}) collective-permute-start(bf16[64,1536]{1,0:T(8,128)(2,1)S(1)} %shard_map.40.refs_0_), channel_id=1, source_target_pairs={{0,1},{1,0},{2,3},{3,2},{4,5},{5,4},{6,7},{7,6},{8,9},{9,8},{10,11... | collective-permute-start | bytes 589832 | tf_op jit(solution)/shard_map/ppermute | solution.py:335
  12.5 1.6 %collective-permute-start.8 = (bf16[64,1536]{1,0:T(8,128)(2,1)S(1)}, bf16[64,1536]{1,0:T(8,128)(2,1)S(1)}, u32[]{:S(2)}, u32[]{:S(2)}) collective-permute-start(bf16[64,1536]{1,0:T(8,128)(2,1)S(1)} %shard_map.40.refs_0_), channel_id=1, source_target_pairs={{0,2},{1,3},{2,0},{3,1},{4,6},{5,7},{6,4},{7,5},{8,10},{9,11},{10,... | collective-permute-start | bytes 589832 | tf_op jit(solution)/shard_map/ppermute | solution.py:338
  14.1 1.5 %collective-permute-start.14 = (bf16[128,1536]{1,0:T(8,128)(2,1)S(1)}, bf16[128,1536]{1,0:T(8,128)(2,1)S(1)}, u32[]{:S(2)}, u32[]{:S(2)}) collective-permute-start(bf16[128,1536]{1,0:T(8,128)(2,1)S(1)} %get-tuple-element.32), channel_id=1, source_target_pairs={{0,16},{8,24},{16,0},{24,8},{1,17},{9,25},{17,1},{25,9},{2,18},{10... | collective-permute-start | bytes 1179656 | tf_op jit(solution)/shard_map/ppermute | solution.py:332
  15.6 0.0 collective-permute-start.9
  15.6 0.5 %collective-permute-start.10 = (bf16[64,1536]{1,0:T(8,128)(2,1)S(1)}, bf16[64,1536]{1,0:T(8,128)(2,1)S(1)}, u32[]{:S(2)}, u32[]{:S(2)}) collective-permute-start(bf16[64,1536]{1,0:T(8,128)(2,1)S(1)} %shard_map.39.refs_1_), channel_id=1, source_target_pairs={{0,8},{8,0},{16,24},{24,16},{1,9},{9,1},{17,25},{25,17},{2,10},{10... | collective-permute-start | bytes 589832 | tf_op jit(solution)/shard_map/ppermute | solution.py:329
  16.1 1.0 %collective-permute-done.7.refs_2_ = bf16[64,1536]{1,0:T(8,128)(2,1)S(1)} collective-permute-done((bf16[64,1536]{1,0:T(8,128)(2,1)S(1)}, bf16[64,1536]{1,0:T(8,128)(2,1)S(1)}, u32[]{:S(2)}, u32[]{:S(2)}) %collective-permute-start.7) | collective-permute-done | bytes 196640 | tf_op jit(solution)/shard_map/ppermute | solution.py:335
  17.1 1.2 %collective-permute-done.8.refs_3_ = bf16[64,1536]{1,0:T(8,128)(2,1)S(1)} collective-permute-done((bf16[64,1536]{1,0:T(8,128)(2,1)S(1)}, bf16[64,1536]{1,0:T(8,128)(2,1)S(1)}, u32[]{:S(2)}, u32[]{:S(2)}) %collective-permute-start.8) | collective-permute-done | bytes 196640 | tf_op jit(solution)/shard_map/ppermute | solution.py:338
  18.4 0.0 collective-permute-start.12
  18.4 0.0 collective-permute-done.9.refs_4_
  18.4 0.8 %collective-permute-start.4 = (bf16[64,1536]{1,0:T(8,128)(2,1)S(1)}, bf16[64,1536]{1,0:T(8,128)(2,1)S(1)}, u32[]{:S(2)}, u32[]{:S(2)}) collective-permute-start(bf16[64,1536]{1,0:T(8,128)(2,1)S(1)} %shard_map.39.refs_1_), channel_id=1, source_target_pairs={{0,1},{1,0},{2,3},{3,2},{4,5},{5,4},{6,7},{7,6},{8,9},{9,8},{10,11... | collective-permute-start | bytes 589832 | tf_op jit(solution)/shard_map/ppermute | solution.py:335
  19.2 0.0 collective-permute-done.10.refs_5_
  19.2 1.6 %collective-permute-start.5 = (bf16[64,1536]{1,0:T(8,128)(2,1)S(1)}, bf16[64,1536]{1,0:T(8,128)(2,1)S(1)}, u32[]{:S(2)}, u32[]{:S(2)}) collective-permute-start(bf16[64,1536]{1,0:T(8,128)(2,1)S(1)} %shard_map.39.refs_1_), channel_id=1, source_target_pairs={{0,2},{1,3},{2,0},{3,1},{4,6},{5,7},{6,4},{7,5},{8,10},{9,11},{10,... | collective-permute-start | bytes 589832 | tf_op jit(solution)/shard_map/ppermute | solution.py:338
  20.7 2.4 %shard_map.41 = (bf16[2048,1024]{1,0:T(8,128)(2,1)S(1)}, bf16[2048,2048]{1,0:T(8,128)(2,1)S(1)}, f32[2048,256]{1,0:T(8,128)S(1)}, bf16[2048,256]{1,0:T(8,128)(2,1)S(1)}, f32[8,128]{1,0:T(8,128)S(1)}) custom-call(bf16[64,1536]{1,0:T(8,128)(2,1)S(1)} %shard_map.40.refs_0_, ...), custom_call_target="tpu_custom_call", output_to_operand_aliasing={{0}: (8, {}), {1}: (9, {}), {2}: (10, {}), {3}: (11, {})} | custom-call | tf_op jit(solution)/shard_map/pallas_call | solution.py:344
  23.2 0.7 %collective-permute-done.14.refs_0_ = bf16[128,1536]{1,0:T(8,128)(2,1)S(1)} collective-permute-done((bf16[128,1536]{1,0:T(8,128)(2,1)S(1)}, bf16[128,1536]{1,0:T(8,128)(2,1)S(1)}, u32[]{:S(2)}, u32[]{:S(2)}) %collective-permute-start.14) | collective-permute-done | bytes 393248 | tf_op jit(solution)/shard_map/ppermute | solution.py:332
  23.9 0.0 collective-permute-start.15
  23.9 1.8 %collective-permute-done.4.refs_0_ = bf16[64,1536]{1,0:T(8,128)(2,1)S(1)} collective-permute-done((bf16[64,1536]{1,0:T(8,128)(2,1)S(1)}, bf16[64,1536]{1,0:T(8,128)(2,1)S(1)}, u32[]{:S(2)}, u32[]{:S(2)}) %collective-permute-start.4) | collective-permute-done | bytes 196640 | tf_op jit(solution)/shard_map/ppermute | solution.py:335
  25.7 0.2 collective-permute-done.5.refs_1_
  25.9 0.1 collective-permute-start.13
  26.0 0.0 collective-permute-done.15.refs_1_
  26.0 1.8 %shard_map.44 = (bf16[2048,1024]{1,0:T(8,128)(2,1)S(1)}, bf16[2048,2048]{1,0:T(8,128)(2,1)S(1)}, f32[2048,256]{1,0:T(8,128)S(1)}, bf16[2048,256]{1,0:T(8,128)(2,1)S(1)}, f32[8,128]{1,0:T(8,128)}) custom-call(bf16[128,1536]{1,0:T(8,128)(2,1)S(1)} %shard_map.43.refs_0_, ...), custom_call_target="tpu_custom_call", output_to_operand_aliasing={{0}: (2, {}), {1}: (3, {}), {2}: (4, {}), {3}: (5, {})} | custom-call | tf_op jit(solution)/shard_map/pallas_call | solution.py:344
  27.8 16.7 %shard_map.45 = f32[64,256]{1,0:T(8,128)} custom-call(bf16[128,1536]{1,0:T(8,128)(2,1)S(1)} %shard_map.42.refs_0_, bf16[128,1536]{1,0:T(8,128)(2,1)S(1)} %collective-permute-done.13.refs_1_, bf16[2048,1024]{1,0:T(8,128)(2,1)S(1)} %get-tuple-element.37.refs_2_, bf16[2048,2048]{1,0:T(8,128)(2,1)S(1)} %get-tuple-element.38.refs_3_, ...), custom_call_target="tpu_custom_call" | custom-call | tf_op jit(solution)/shard_map/pallas_call | solution.py:390
  (9 shorter events, 0.0 us)
Async XLA Ops:
  0.0 4.9 %collective-permute-start.1 = (bf16[2,512,256]{2,1,0:T(8,128)(2,1)}, bf16[2,512,256]{2,1,0:T(8,128)(2,1)S(1)}, u32[]{:S(2)}, u32[]{:S(2)}) collective-permute-start(bf16[2,512,256]{2,1,0:T(8,128)(2,1)} %refs_0_.1), channel_id=1, source_target_pairs={{0,8},{8,0},{16,24},{24,16},{1,9},{9,1},{17,25},{25,17},{2,10},{10... | collective-permute-start | bytes 1572872 | tf_op jit(solution)/shard_map/ppermute | solution.py:329
  0.5 4.4 %collective-permute-start.2 = (bf16[2,512,256]{2,1,0:T(8,128)(2,1)}, bf16[2,512,256]{2,1,0:T(8,128)(2,1)S(1)}, u32[]{:S(2)}, u32[]{:S(2)}) collective-permute-start(bf16[2,512,256]{2,1,0:T(8,128)(2,1)} %refs_1_.1), channel_id=1, source_target_pairs={{0,8},{8,0},{16,24},{24,16},{1,9},{9,1},{17,25},{25,17},{2,10},{10... | collective-permute-start | bytes 1572872 | tf_op jit(solution)/shard_map/ppermute | solution.py:329
  0.5 4.4 %collective-permute-start.3 = (f32[512,256]{1,0:T(8,128)}, f32[512,256]{1,0:T(8,128)S(1)}, u32[]{:S(2)}, u32[]{:S(2)}) collective-permute-start(f32[512,256]{1,0:T(8,128)} %refs_2_.1), channel_id=1, source_target_pairs={{0,8},{8,0},{16,24},{24,16},{1,9},{9,1},{17,25},{25,17},{2,10},{10... | collective-permute-start | bytes 1572872 | tf_op jit(solution)/shard_map/ppermute | solution.py:329
  2.2 8.3 %collective-permute-start.6 = (bf16[64,1536]{1,0:T(8,128)(2,1)S(1)}, bf16[64,1536]{1,0:T(8,128)(2,1)S(1)}, u32[]{:S(2)}, u32[]{:S(2)}) collective-permute-start(bf16[64,1536]{1,0:T(8,128)(2,1)S(1)} %get-tuple-element.26), channel_id=1, source_target_pairs={{0,16},{8,24},{16,0},{24,8},{1,17},{9,25},{17,1},{25,9},{2,18},{10... | collective-permute-start | bytes 589832 | tf_op jit(solution)/shard_map/ppermute | solution.py:332
  4.8 10.8 %collective-permute-start = (bf16[64,1536]{1,0:T(8,128)(2,1)S(1)}, bf16[64,1536]{1,0:T(8,128)(2,1)S(1)}, u32[]{:S(2)}, u32[]{:S(2)}) collective-permute-start(bf16[64,1536]{1,0:T(8,128)(2,1)S(1)} %get-tuple-element.23), channel_id=1, source_target_pairs={{0,16},{8,24},{16,0},{24,8},{1,17},{9,25},{17,1},{25,9},{2,18},{10... | collective-permute-start | bytes 589832 | tf_op jit(solution)/shard_map/ppermute | solution.py:332
  10.6 6.6 %collective-permute-start.7 = (bf16[64,1536]{1,0:T(8,128)(2,1)S(1)}, bf16[64,1536]{1,0:T(8,128)(2,1)S(1)}, u32[]{:S(2)}, u32[]{:S(2)}) collective-permute-start(bf16[64,1536]{1,0:T(8,128)(2,1)S(1)} %shard_map.40.refs_0_), channel_id=1, source_target_pairs={{0,1},{1,0},{2,3},{3,2},{4,5},{5,4},{6,7},{7,6},{8,9},{9,8},{10,11... | collective-permute-start | bytes 589832 | tf_op jit(solution)/shard_map/ppermute | solution.py:335
  12.5 5.9 %collective-permute-start.8 = (bf16[64,1536]{1,0:T(8,128)(2,1)S(1)}, bf16[64,1536]{1,0:T(8,128)(2,1)S(1)}, u32[]{:S(2)}, u32[]{:S(2)}) collective-permute-start(bf16[64,1536]{1,0:T(8,128)(2,1)S(1)} %shard_map.40.refs_0_), channel_id=1, source_target_pairs={{0,2},{1,3},{2,0},{3,1},{4,6},{5,7},{6,4},{7,5},{8,10},{9,11},{10,... | collective-permute-start | bytes 589832 | tf_op jit(solution)/shard_map/ppermute | solution.py:338
  14.1 9.8 %collective-permute-start.14 = (bf16[128,1536]{1,0:T(8,128)(2,1)S(1)}, bf16[128,1536]{1,0:T(8,128)(2,1)S(1)}, u32[]{:S(2)}, u32[]{:S(2)}) collective-permute-start(bf16[128,1536]{1,0:T(8,128)(2,1)S(1)} %get-tuple-element.32), channel_id=1, source_target_pairs={{0,16},{8,24},{16,0},{24,8},{1,17},{9,25},{17,1},{25,9},{2,18},{10... | collective-permute-start | bytes 1179656 | tf_op jit(solution)/shard_map/ppermute | solution.py:332
  15.6 2.8 %collective-permute-start.9 = (bf16[64,1536]{1,0:T(8,128)(2,1)S(1)}, bf16[64,1536]{1,0:T(8,128)(2,1)S(1)}, u32[]{:S(2)}, u32[]{:S(2)}) collective-permute-start(bf16[64,1536]{1,0:T(8,128)(2,1)S(1)} %shard_map.40.refs_0_), channel_id=1, source_target_pairs={{0,8},{8,0},{16,24},{24,16},{1,9},{9,1},{17,25},{25,17},{2,10},{10... | collective-permute-start | bytes 589832 | tf_op jit(solution)/shard_map/ppermute | solution.py:329
  15.6 3.6 %collective-permute-start.10 = (bf16[64,1536]{1,0:T(8,128)(2,1)S(1)}, bf16[64,1536]{1,0:T(8,128)(2,1)S(1)}, u32[]{:S(2)}, u32[]{:S(2)}) collective-permute-start(bf16[64,1536]{1,0:T(8,128)(2,1)S(1)} %shard_map.39.refs_1_), channel_id=1, source_target_pairs={{0,8},{8,0},{16,24},{24,16},{1,9},{9,1},{17,25},{25,17},{2,10},{10... | collective-permute-start | bytes 589832 | tf_op jit(solution)/shard_map/ppermute | solution.py:329
  17.1 3.6 %collective-permute-start.11 = (bf16[64,1536]{1,0:T(8,128)(2,1)S(1)}, bf16[64,1536]{1,0:T(8,128)(2,1)S(1)}, u32[]{:S(2)}, u32[]{:S(2)}) collective-permute-start(bf16[64,1536]{1,0:T(8,128)(2,1)S(1)} %collective-permute-done.7.refs_2_), channel_id=1, source_target_pairs={{0,8},{8,0},{16,24},{24,16},{1,9},{9,1},{17,25},{25,17},{2,10},{10... | collective-permute-start | bytes 589832 | tf_op jit(solution)/shard_map/ppermute | solution.py:329
  18.4 2.4 %collective-permute-start.12 = (bf16[64,1536]{1,0:T(8,128)(2,1)S(1)}, bf16[64,1536]{1,0:T(8,128)(2,1)S(1)}, u32[]{:S(2)}, u32[]{:S(2)}) collective-permute-start(bf16[64,1536]{1,0:T(8,128)(2,1)S(1)} %collective-permute-done.8.refs_3_), channel_id=1, source_target_pairs={{0,8},{8,0},{16,24},{24,16},{1,9},{9,1},{17,25},{25,17},{2,10},{10... | collective-permute-start | bytes 589832 | tf_op jit(solution)/shard_map/ppermute | solution.py:329
  18.4 7.3 %collective-permute-start.4 = (bf16[64,1536]{1,0:T(8,128)(2,1)S(1)}, bf16[64,1536]{1,0:T(8,128)(2,1)S(1)}, u32[]{:S(2)}, u32[]{:S(2)}) collective-permute-start(bf16[64,1536]{1,0:T(8,128)(2,1)S(1)} %shard_map.39.refs_1_), channel_id=1, source_target_pairs={{0,1},{1,0},{2,3},{3,2},{4,5},{5,4},{6,7},{7,6},{8,9},{9,8},{10,11... | collective-permute-start | bytes 589832 | tf_op jit(solution)/shard_map/ppermute | solution.py:335
  19.2 6.8 %collective-permute-start.5 = (bf16[64,1536]{1,0:T(8,128)(2,1)S(1)}, bf16[64,1536]{1,0:T(8,128)(2,1)S(1)}, u32[]{:S(2)}, u32[]{:S(2)}) collective-permute-start(bf16[64,1536]{1,0:T(8,128)(2,1)S(1)} %shard_map.39.refs_1_), channel_id=1, source_target_pairs={{0,2},{1,3},{2,0},{3,1},{4,6},{5,7},{6,4},{7,5},{8,10},{9,11},{10,... | collective-permute-start | bytes 589832 | tf_op jit(solution)/shard_map/ppermute | solution.py:338
  23.9 2.2 %collective-permute-start.15 = (bf16[128,1536]{1,0:T(8,128)(2,1)S(1)}, bf16[128,1536]{1,0:T(8,128)(2,1)S(1)}, u32[]{:S(2)}, u32[]{:S(2)}) collective-permute-start(bf16[128,1536]{1,0:T(8,128)(2,1)S(1)} %shard_map.43.refs_0_), channel_id=1, source_target_pairs={{0,8},{8,0},{16,24},{24,16},{1,9},{9,1},{17,25},{25,17},{2,10},{10... | collective-permute-start | bytes 1179656 | tf_op jit(solution)/shard_map/ppermute | solution.py:329
  25.9 1.8 %collective-permute-start.13 = (bf16[128,1536]{1,0:T(8,128)(2,1)S(1)}, bf16[128,1536]{1,0:T(8,128)(2,1)S(1)}, u32[]{:S(2)}, u32[]{:S(2)}) collective-permute-start(bf16[128,1536]{1,0:T(8,128)(2,1)S(1)} %shard_map.42.refs_0_), channel_id=1, source_target_pairs={{0,8},{8,0},{16,24},{24,16},{1,9},{9,1},{17,25},{25,17},{2,10},{10... | collective-permute-start | bytes 1179656 | tf_op jit(solution)/shard_map/ppermute | solution.py:329
